TPU v7x, 1024 devices: a whole 4x8x16 slice. The times are simulated.
1024 devices in a mesh: dp: 128 (over y, z_hi, x, core), tensor: 8 (over z_lo).
Axes of the slice: x: 4, y: 8, z: 16 (z_hi: 2, z_lo: 8; z = z_hi * 8 + z_lo), core: 2. Of those that a mesh axis runs over, the one named last changes fastest.
Arguments:
- cache_keys: bfloat16 [512, 1536, 1024], P('dp', None, 'tensor'), may hold values from -6 to 6
- cache_values: bfloat16 [512, 1536, 1024], P('dp', None, 'tensor'), may hold values from -6 to 6
- lengths: int32 [512], P('dp'), may hold values from 1 to 3, as said below
- finished: int32 [512], P('dp'), may hold values from 0 to 1, as said below
- migrations: int32 [64, 4], replicated, may hold values from 0 to 127, as said below
- queries: bfloat16 [8, 512, 8192], P(None, 'dp', 'tensor'), may hold values from -6 to 6
- new_keys: bfloat16 [8, 512, 1024], P(None, 'dp', 'tensor'), may hold values from -6 to 6
- new_values: bfloat16 [8, 512, 1024], P(None, 'dp', 'tensor'), may hold values from -6 to 6
- out_weight: bfloat16 [8192, 2560], P('tensor'), may hold values from -0.5 to 0.5
Outputs:
- output: bfloat16 [8, 512, 2560], P(None, 'dp')
Inputs may be any that keep to these rules, and one draw needn't show every extreme that they name: `lengths`: whole blocks of 512 tokens; some row holds 3 blocks in every draw. `finished`: 1 marks a row whose generation has ended; its slot is free. `migrations`: each entry moves one row to the next group, (source + 1) modulo the number of groups. No group is a source twice or a destination twice, and no group is both. The moved row is unfinished and the destination slot is finished.
All inputs are finite; a program needn't handle non-finite values.
Results may differ from a plain program's by a relative error of at most 0.0054.
Values may be sent and summed in bfloat16 or wider, within the bound.
A program may use at most 32 MiB of HBM per device.

v0:
```python
import jax
import jax.numpy as jnp
from jax import lax
from jax.sharding import PartitionSpec as P

HD = 128
BLOCK = 512


def from_behind(value, axis, steps):
    count = lax.axis_size(axis)
    pairs = [(source, (source + steps) % count) for source in range(count)]
    return lax.ppermute(value, axis, pairs)


def attend(queries, fresh_keys, fresh_values, key_cache, value_cache, blocks):
    step_count = queries.shape[0]
    row_count = queries.shape[1]
    cache_len = key_cache.shape[1]
    local_groups = fresh_keys.shape[2] // HD
    grouping = queries.shape[2] // HD // local_groups
    score_scale = 1.0 / HD**0.5
    query_heads = queries.reshape(step_count, row_count, local_groups, grouping, HD)
    key_heads = key_cache.reshape(row_count, cache_len, local_groups, HD)
    value_heads = value_cache.reshape(row_count, cache_len, local_groups, HD)
    fresh_key_heads = fresh_keys.reshape(step_count, row_count, local_groups, HD)
    fresh_value_heads = fresh_values.reshape(step_count, row_count, local_groups, HD)
    cached_scores = (
        jnp.einsum("srkgd,rckd->rksgc", query_heads, key_heads, preferred_element_type=jnp.float32)
        * score_scale
    )
    fresh_scores = (
        jnp.einsum(
            "srkgd,urkd->rksgu", query_heads, fresh_key_heads, preferred_element_type=jnp.float32
        )
        * score_scale
    )
    cache_mask = (jnp.arange(cache_len, dtype=jnp.int32)[None, :] < blocks[:, None] * BLOCK)[
        :, None, None, None, :
    ]
    step_ids = jnp.arange(step_count, dtype=jnp.int32)
    fresh_mask = (step_ids[None, :] <= step_ids[:, None])[None, None, :, None, :]
    cached_scores = jnp.where(cache_mask, cached_scores, -1e30)
    fresh_scores = jnp.where(fresh_mask, fresh_scores, -1e30)
    peak_score = jnp.maximum(jnp.max(cached_scores, axis=4), jnp.max(fresh_scores, axis=4))[
        ..., None
    ]
    cached_weights = jnp.exp(cached_scores - peak_score)
    fresh_weights = jnp.exp(fresh_scores - peak_score)
    totals = jnp.sum(cached_weights, axis=4) + jnp.sum(fresh_weights, axis=4)
    mixed_out = jnp.einsum(
        "rksgc,rckd->srkgd",
        cached_weights.astype(jnp.bfloat16),
        value_heads,
        preferred_element_type=jnp.float32,
    )
    mixed_out = mixed_out + jnp.einsum(
        "rksgu,urkd->srkgd",
        fresh_weights.astype(jnp.bfloat16),
        fresh_value_heads,
        preferred_element_type=jnp.float32,
    )
    normaliser = jnp.transpose(totals, (2, 0, 1, 3))[..., None]
    return (
        (mixed_out / normaliser)
        .astype(jnp.bfloat16)
        .reshape(step_count, row_count, local_groups * grouping * HD)
    )


def per_device(
    cache_keys,
    cache_values,
    lengths,
    finished,
    migrations,
    queries,
    new_keys,
    new_values,
    out_weight,
):
    row_count = cache_keys.shape[0]
    group_index = lax.axis_index("dp")
    sending = migrations[:, 0] == group_index
    arriving = migrations[:, 1] == group_index
    has_send = jnp.any(sending)
    has_arrival = jnp.any(arriving)
    sent_row = jnp.sum(jnp.where(sending, migrations[:, 2], 0))
    arrival_slot = jnp.sum(jnp.where(arriving, migrations[:, 3], 0))
    row_ids = jnp.arange(row_count, dtype=jnp.int32)
    moved_away = has_send & (row_ids == sent_row)
    staying = (finished == 0) & jnp.logical_not(moved_away)
    incoming = has_arrival & (row_ids == arrival_slot)
    arrival_query = lax.dynamic_slice_in_dim(queries, arrival_slot, 1, 1)
    arrival_keys = lax.dynamic_slice_in_dim(new_keys, arrival_slot, 1, 1)
    arrival_values = lax.dynamic_slice_in_dim(new_values, arrival_slot, 1, 1)
    moved_keys = lax.dynamic_slice_in_dim(cache_keys, sent_row, 1, 0)
    moved_values = lax.dynamic_slice_in_dim(cache_values, sent_row, 1, 0)
    moved_blocks = lax.dynamic_slice_in_dim(lengths, sent_row, 1, 0).astype(jnp.bfloat16)
    got_keys, got_values, got_blocks = from_behind(
        (moved_keys, moved_values, moved_blocks), "dp", 1
    )
    resident = attend(queries, new_keys, new_values, cache_keys, cache_values, lengths)
    arrived = attend(
        arrival_query,
        arrival_keys,
        arrival_values,
        got_keys,
        got_values,
        got_blocks.astype(jnp.int32),
    )
    attended = jnp.where(
        incoming[None, :, None],
        arrived,
        jnp.where(staying[None, :, None], resident, jnp.zeros_like(resident)),
    )
    partial_out = jnp.dot(
        attended.reshape(-1, attended.shape[2]), out_weight, preferred_element_type=jnp.float32
    )
    summed = lax.psum(partial_out, "tensor")
    return summed.astype(jnp.bfloat16).reshape(attended.shape[0], row_count, out_weight.shape[1])


def solution(mesh):
    return jax.shard_map(
        per_device,
        mesh=mesh,
        in_specs=(
            P("dp", None, "tensor"),
            P("dp", None, "tensor"),
            P("dp"),
            P("dp"),
            P(),
            P(None, "dp", "tensor"),
            P(None, "dp", "tensor"),
            P(None, "dp", "tensor"),
            P("tensor", None),
        ),
        out_specs=P(None, "dp", None),
        check_vma=False,
    )
```

profile of v0, /device:TPU:32, one launch (start us, length us, event | category | flops | bytes accessed | tf_op | source)
XLA Modules:
  0.0 134.8 jit_solution(3342817664751870590)
XLA Ops:
  0.0 0.0 copy-start
  0.0 0.0 copy-start.4
  0.0 0.0 copy-start.7
  0.0 0.0 copy-start.2
  0.0 0.0 copy-start.3
  0.0 1.5 %fusion.59 = (s32[]{:T(128)}, s32[]{:T(128)}) fusion(s32[64,4]{0,1:T(4,128)} %param.13, s32[]{:T(128)S(6)} %axis_index.15), kind=kLoop, calls=%fused_computation.74 | loop fusion | flops 382 | bytes 1036 | tf_op jit(solution)/shard_map/reduce_sum | solution.py:88
  3.5 1.3 dynamic_slice.19
  5.4 2.9 %collective-permute-start.1 = (bf16[1]{0:T(256)(128)(2,1)}, bf16[1]{0:T(256)(128)(2,1)}, u32[]{:S(2)}, u32[]{:S(2)}) collective-permute-start(bf16[1]{0:T(256)(128)(2,1)} %convert_element_type.34), channel_id=1, source_target_pairs={{0,8},{8,16},{16,24},{24,32},{32,40},{40,48},{48,56},{56,64},{64,7... | collective-permute-start | bytes 14 | tf_op jit(solution)/shard_map/ppermute | solution.py:13
  8.3 1.0 constant_dynamic-slice_fusion.3
  9.3 3.3 %collective-permute-start = (bf16[1,1536,128]{2,1,0:T(8,128)(2,1)S(1)}, bf16[1,1536,128]{2,1,0:T(8,128)(2,1)S(1)}, u32[]{:S(2)}, u32[]{:S(2)}) collective-permute-start(bf16[1,1536,128]{2,1,0:T(8,128)(2,1)S(1)} %constant_dynamic-slice_fusion.3), channel_id=1, source_target_pairs={{0,8},{8,16},{16,24},{24,32},{32,40},{40,48},{48,56},{56,64},{64,7... | collective-permute-start | bytes 1179656 | tf_op jit(solution)/shard_map/ppermute | solution.py:13
  12.6 0.0 copy-done
  12.6 2.1 %collective-permute-start.2 = (bf16[1,1536,128]{2,1,0:T(8,128)(2,1)S(1)}, bf16[1,1536,128]{2,1,0:T(8,128)(2,1)S(1)}, u32[]{:S(2)}, u32[]{:S(2)}) collective-permute-start(bf16[1,1536,128]{2,1,0:T(8,128)(2,1)S(1)} %constant_dynamic-slice_fusion.2), channel_id=1, source_target_pairs={{0,8},{8,16},{16,24},{24,32},{32,40},{40,48},{48,56},{56,64},{64,7... | collective-permute-start | bytes 1179656 | tf_op jit(solution)/shard_map/ppermute | solution.py:13
  14.8 0.0 copy-done.7
  15.9 0.0 copy-done.4
  15.9 0.7 compare_reduce_fusion.1
  16.6 0.1 iota_compare_fusion
  16.7 0.0 copy-done.2
  17.3 0.0 copy-done.3
  17.4 0.0 copy-start.5
  17.4 0.7 fusion.63
  18.1 0.0 copy-start.1
  18.1 0.0 copy-done.5
  18.1 0.4 fusion.64
  18.6 0.1 fusion.33
  18.6 0.2 fusion.35
  18.9 0.4 fusion.5
  19.2 0.3 copy-done.1
  19.5 0.0 copy-start.6
  19.5 0.5 fusion.22
  20.0 0.2 copy-done.6
  20.2 2.4 %not_and_fusion = (pred[4]{0:T(512)(128)(4,1)S(1)}, pred[4]{0:T(512)(128)(4,1)S(1)}) fusion(s32[4]{0:T(128)S(1)} %copy-done.6, pred[]{:T(512)} %get-tuple-element.6, s32[]{:T(128)} %get-tuple-element.7, s32[]{:T(128)} %get-tuple-element.8, pred[]{:T(512)} %get-tuple-element.5), kind=kLoop, calls=%fused_computation.63 | loop fusion | flops 28 | bytes 34 | tf_op jit(solution)/shard_map/and | solution.py:92
  22.7 0.1 broadcast_in_dim.121
  22.8 0.1 broadcast_in_dim.111
  22.9 0.1 dynamic-slice_reduce_fusion
  23.0 0.2 fusion.62
  23.2 4.4 %collective-permute-done.1 = bf16[1]{0:T(256)(128)(2,1)} collective-permute-done((bf16[1]{0:T(256)(128)(2,1)}, bf16[1]{0:T(256)(128)(2,1)}, u32[]{:S(2)}, u32[]{:S(2)}) %collective-permute-start.1) | collective-permute-done | bytes 34 | tf_op jit(solution)/shard_map/ppermute | solution.py:13
  28.3 11.6 %collective-permute-done.2 = bf16[1,1536,128]{2,1,0:T(8,128)(2,1)S(1)} collective-permute-done((bf16[1,1536,128]{2,1,0:T(8,128)(2,1)S(1)}, bf16[1,1536,128]{2,1,0:T(8,128)(2,1)S(1)}, u32[]{:S(2)}, u32[]{:S(2)}) %collective-permute-start.2) | collective-permute-done | bytes 393248 | tf_op jit(solution)/shard_map/ppermute | solution.py:13
  39.9 0.3 fusion.61
  40.3 0.2 fusion.29
  40.5 0.2 fusion.49
  40.7 0.0 collective-permute-done
  40.7 0.3 fusion.18
  41.0 3.5 %fusion.38 = f32[32,2560]{1,0:T(8,128)S(1)} fusion(bf16[1024,2560]{1,0:T(8,128)(2,1)} %param.17, bf16[32,1024]{1,0:T(8,128)(2,1)S(1)} %broadcast_in_dim.119, bf16[4,8,8,128]{3,2,1,0:T(8,128)(2,1)S(1)} %bitcast.94, pred[32]{0:T(512)(128)(4,1)S(1)} %broadcast_in_dim.121, pred[32]{0:T(512)(128)(4,1)S(1)} %broadcast_in_dim.111), kind=kOutput, calls=%fused_computation.36 | convolution fusion | flops 167837696 | bytes 5701696 | tf_op jit(solution)/shard_map/dot_general | solution.py:117
  44.6 89.5 %all-reduce.1 = bf16[32,2560]{1,0:T(8,128)(2,1)S(1)} all-reduce(f32[32,2560]{1,0:T(8,128)S(1)} %fusion.38), channel_id=1, replica_groups=mesh['dp'=128,'tensor'=8] {'tensor'}, use_global_device_ids=true, to_apply=%region_12.13 | all-reduce | flops 81920 | bytes 491520 | tf_op jit(solution)/shard_map/psum | solution.py:120
  134.0 0.7 reshape.228
  (18 shorter events, 0.2 us)
Async XLA Ops:
  0.0 12.6 %copy-start = (bf16[4,1536,128]{2,1,0:T(8,128)(2,1)S(1)}, bf16[4,1536,128]{2,1,0:T(8,128)(2,1)}, u32[]{:S(2)}) copy-start(bf16[4,1536,128]{2,1,0:T(8,128)(2,1)} %param.9) | copy-start | bytes 4718596
  0.0 15.9 %copy-start.4 = (s32[64,4]{0,1:T(4,128)S(1)}, s32[64,4]{0,1:T(4,128)}, u32[]{:S(2)}) copy-start(s32[64,4]{0,1:T(4,128)} %param.13) | copy-start | bytes 3076
  0.0 14.8 %copy-start.7 = (s32[4]{0:T(128)S(1)}, s32[4]{0:T(128)}, u32[]{:S(2)}) copy-start(s32[4]{0:T(128)} %param.11) | copy-start | bytes 52
  0.0 16.7 %copy-start.2 = (bf16[8,4,1024]{2,1,0:T(4,128)(2,1)S(1)}, bf16[8,4,1024]{2,1,0:T(4,128)(2,1)}, u32[]{:S(2)}) copy-start(bf16[8,4,1024]{2,1,0:T(4,128)(2,1)} %param.14) | copy-start | bytes 196612
  0.0 17.3 %copy-start.3 = (bf16[8,4,128]{2,1,0:T(4,128)(2,1)S(1)}, bf16[8,4,128]{2,1,0:T(4,128)(2,1)}, u32[]{:S(2)}) copy-start(bf16[8,4,128]{2,1,0:T(4,128)(2,1)} %param.16) | copy-start | bytes 24580
  5.4 22.2 %collective-permute-start.1 = (bf16[1]{0:T(256)(128)(2,1)}, bf16[1]{0:T(256)(128)(2,1)}, u32[]{:S(2)}, u32[]{:S(2)}) collective-permute-start(bf16[1]{0:T(256)(128)(2,1)} %convert_element_type.34), channel_id=1, source_target_pairs={{0,8},{8,16},{16,24},{24,32},{32,40},{40,48},{48,56},{56,64},{64,7... | collective-permute-start | bytes 14 | tf_op jit(solution)/shard_map/ppermute | solution.py:13
  9.3 31.4 %collective-permute-start = (bf16[1,1536,128]{2,1,0:T(8,128)(2,1)S(1)}, bf16[1,1536,128]{2,1,0:T(8,128)(2,1)S(1)}, u32[]{:S(2)}, u32[]{:S(2)}) collective-permute-start(bf16[1,1536,128]{2,1,0:T(8,128)(2,1)S(1)} %constant_dynamic-slice_fusion.3), channel_id=1, source_target_pairs={{0,8},{8,16},{16,24},{24,32},{32,40},{40,48},{48,56},{56,64},{64,7... | collective-permute-start | bytes 1179656 | tf_op jit(solution)/shard_map/ppermute | solution.py:13
  12.6 27.3 %collective-permute-start.2 = (bf16[1,1536,128]{2,1,0:T(8,128)(2,1)S(1)}, bf16[1,1536,128]{2,1,0:T(8,128)(2,1)S(1)}, u32[]{:S(2)}, u32[]{:S(2)}) collective-permute-start(bf16[1,1536,128]{2,1,0:T(8,128)(2,1)S(1)} %constant_dynamic-slice_fusion.2), channel_id=1, source_target_pairs={{0,8},{8,16},{16,24},{24,32},{32,40},{40,48},{48,56},{56,64},{64,7... | collective-permute-start | bytes 1179656 | tf_op jit(solution)/shard_map/ppermute | solution.py:13
  17.4 0.8 copy-start.5
  18.1 1.4 %copy-start.1 = (bf16[4,1536,128]{2,1,0:T(8,128)(2,1)S(1)}, bf16[4,1536,128]{2,1,0:T(8,128)(2,1)}, u32[]{:S(2)}) copy-start(bf16[4,1536,128]{2,1,0:T(8,128)(2,1)} %param.10) | copy-start | bytes 4718596
  19.5 0.7 copy-start.6
where the time goes:
time: 135 us
  blocking collectives  89.5 us (66%)
  waiting for transfers between devices  16.1 us (12%)
  starting transfers between devices  8.28 us (6%)
  matrix products  6.4 us (5%)
  other arithmetic  5.44 us (4%)
  between operations  5.19 us (4%)
  local copies, waits for them, and re-layouts  3.95 us (3%)
    psum x1, blocking collectives, per_device(): summed = lax.psum(partial_out, 'tensor')  89.5 us
    ppermute x3, waiting for transfers between devices, from_behind(): return lax.ppermute(value, axis, pairs)  16.1 us
    ppermute x3, starting transfers between devices, from_behind(): return lax.ppermute(value, axis, pairs)  8.28 us
    dot_general x1, matrix products, per_device(): jnp.dot(attended.reshape(-1, attended.shape[2]), out_weight, preferred_el...  3.54 us
  transfers between devices with their start and end apart: 3, of which 2 were waited for; matrix products, arithmetic and copies ran while one was open for 6% of the time, Pallas kernels for 0%

commit v1 on v0

v1 whole, which is shorter than its diff:
```python
import functools

import jax
import jax.numpy as jnp
from jax import lax
from jax.experimental import pallas as pl
from jax.experimental.pallas import tpu as pltpu
from jax.sharding import PartitionSpec as P

HD = 128
BLOCK = 512
LANES = 128
MESH = pl.DeviceIdType.MESH
F32 = jnp.float32
BF16 = jnp.bfloat16


def one_hot(mask):
    return jnp.where(mask, 1.0, 0.0).astype(BF16)


def grid_ids(shape):
    return (
        lax.broadcasted_iota(jnp.int32, shape, 0),
        lax.broadcasted_iota(jnp.int32, shape, 1),
    )


def dot(a, b):
    return lax.dot_general(a, b, (((1,), (0,)), ((), ())), preferred_element_type=F32)


def dot_t(a, b):
    return lax.dot_general(a, b, (((1,), (1,)), ((), ())), preferred_element_type=F32)


def stack_heads(rows, heads):
    return jnp.concatenate([rows[:, h * HD : (h + 1) * HD] for h in range(heads)], axis=0)


def attend(query, keys, values, fresh_keys, fresh_values, limit, steps, heads):
    scale = 1.0 / HD**0.5
    scores = dot_t(query, keys) * scale
    fresh = dot_t(query, fresh_keys) * scale
    _, position = grid_ids(scores.shape)
    scores = jnp.where(position < limit, scores, -1e30)
    row, token = grid_ids(fresh.shape)
    fresh = jnp.where(token <= lax.rem(row, steps), fresh, -1e30)
    peak = jnp.maximum(
        jnp.max(scores, axis=1, keepdims=True), jnp.max(fresh, axis=1, keepdims=True)
    )
    weights = jnp.exp(scores - peak)
    fresh_weights = jnp.exp(fresh - peak)
    total = jnp.sum(weights, axis=1, keepdims=True) + jnp.sum(fresh_weights, axis=1, keepdims=True)
    mixed = dot(weights.astype(BF16), values) + dot(fresh_weights.astype(BF16), fresh_values)
    mixed = mixed / total
    return jnp.concatenate([mixed[h * steps : (h + 1) * steps] for h in range(heads)], axis=1)


def kernel(
    lengths, finished, mig, query, fresh, keys_hbm, values_hbm, weight_hbm,
    out,
    keys, values, weight, ask, asked, part, reduced, moved_part, moved_in, chunk, gathered,
    load_sem, ask_send, ask_recv, rs_send, rs_recv, mv_send, mv_recv, ag_send, ag_recv,
    *, slots, steps, heads, n_dp, n_t,
):
    g, t = lax.axis_index("dp"), lax.axis_index("tensor")
    up, down = lax.rem(g + 1, n_dp), lax.rem(g + n_dp - 1, n_dp)
    rows = slots * steps

    barrier = pltpu.get_barrier_semaphore()
    for p in range(1, n_t):
        pl.semaphore_signal(barrier, inc=1, device_id=(g, lax.rem(t + p, n_t)), device_id_type=MESH)
    for p in range(n_t):
        other = lax.rem(t + p, n_t)
        pl.semaphore_signal(barrier, inc=1, device_id=(up, other), device_id_type=MESH)
        pl.semaphore_signal(barrier, inc=1, device_id=(down, other), device_id_type=MESH)

    loads = [
        pltpu.make_async_copy(src, dst, load_sem.at[i])
        for i, (src, dst) in enumerate(
            [(keys_hbm, keys), (values_hbm, values), (weight_hbm, weight)]
        )
    ]
    for load in loads:
        load.start()

    sending = mig[0:1, :] == g
    arriving = mig[1:2, :] == g
    has_send = jnp.sum(sending.astype(jnp.int32)) > 0
    has_arrival = jnp.sum(arriving.astype(jnp.int32)) > 0
    sent_row = jnp.sum(jnp.where(sending, mig[2:3, :], 0))
    arrival_slot = jnp.sum(jnp.where(arriving, mig[3:4, :], 0))

    i, j = grid_ids((rows + steps, rows))
    slot = jnp.where(i < rows, i // steps, arrival_slot)
    order = one_hot(j == lax.rem(i, steps) * slots + slot)
    by_slot = dot(order, query[...])
    fresh_by_slot = dot(order, fresh[...])
    ask[0 : heads * steps, :] = stack_heads(by_slot[rows:], heads).astype(BF16)
    ask[heads * steps :, :] = stack_heads(fresh_by_slot[rows:], 2).astype(BF16)

    zeros = jnp.zeros((16 - steps, HD), F32)

    def pad(x):
        return jnp.concatenate([x, zeros], axis=0).astype(BF16)

    loads[0].wait()
    loads[1].wait()
    attended = []
    for r in range(slots):
        mine = slice(r * steps, (r + 1) * steps)
        mixed = attend(
            stack_heads(by_slot[mine], heads).astype(BF16),
            keys[r], values[r],
            pad(fresh_by_slot[mine, :HD]), pad(fresh_by_slot[mine, HD:]),
            lengths[r] * BLOCK, steps, heads,
        )
        stays = jnp.logical_and(
            finished[r] == 0, jnp.logical_not(jnp.logical_and(has_send, sent_row == r))
        )
        attended.append(jnp.where(stays, mixed, 0.0))
    attended = jnp.concatenate(attended, axis=0).astype(BF16)
    i, j = grid_ids((rows, rows))
    to_steps = one_hot(j == lax.rem(i, slots) * steps + i // slots)
    attended = dot(to_steps, attended).astype(BF16)

    loads[2].wait()
    half = rows // 2
    for c in range(10):
        block = dot(attended, weight[:, 256 * c : 256 * (c + 1)]).astype(BF16)
        for k in range(2):
            for h in range(2):
                piece = block[h * half : (h + 1) * half, k * LANES : (k + 1) * LANES]
                if c < 8:
                    part[c, 2 * k + h] = piece
                else:
                    part[2 * (2 * (c - 8) + k) + h, 4] = piece

    pl.semaphore_wait(barrier, 3 * n_t - 1)
    ask_copy = pltpu.make_async_remote_copy(
        ask, asked, ask_send, ask_recv, device_id=(down, t), device_id_type=MESH
    )
    ask_copy.start()

    def rs_copy(j, slot):
        return pltpu.make_async_remote_copy(
            part.at[j], reduced.at[slot], rs_send.at[j], rs_recv.at[slot],
            device_id=(g, j), device_id_type=MESH,
        )

    peers = [lax.rem(t + p, n_t) for p in range(1, n_t)]
    for j in peers:
        rs_copy(j, t).start()

    ask_copy.wait_recv()
    asked_fresh = asked[heads * steps :, :].astype(F32)
    moved = attend(
        asked[0 : heads * steps, :],
        keys[sent_row], values[sent_row],
        pad(asked_fresh[:steps]), pad(asked_fresh[steps:]),
        lengths[sent_row] * BLOCK, steps, heads,
    )
    moved = jnp.where(has_send, moved, 0.0).astype(BF16)
    for c in range(10):
        block = dot(moved, weight[:, 256 * c : 256 * (c + 1)])
        piece = jnp.concatenate([block[:, :LANES], block[:, LANES:]], axis=0).astype(BF16)
        if c < 8:
            moved_part[c, 0] = piece
        else:
            for j in range(4):
                moved_part[4 * (c - 8) + j, 1] = piece

    def mv_copy(group, j, slot):
        return pltpu.make_async_remote_copy(
            moved_part.at[j], moved_in.at[slot], mv_send.at[j], mv_recv.at[slot],
            device_id=(group, j), device_id_type=MESH,
        )

    for p in range(n_t):
        mv_copy(up, lax.rem(t + p, n_t), t).start()

    total = part[t].astype(F32)
    for j in peers:
        rs_copy(j, j).wait_recv()
        total = total + reduced[j].astype(F32)
    arrived = None
    for p in range(n_t):
        j = lax.rem(t + p, n_t)
        mv_copy(up, j, j).wait_recv()
        piece = moved_in[j].astype(F32)
        arrived = piece if arrived is None else arrived + piece
    arrived = jnp.where(has_arrival, arrived, 0.0).astype(BF16)
    i, j = grid_ids((rows, steps))
    place = one_hot(jnp.logical_and(lax.rem(i, slots) == arrival_slot, i // slots == j))
    lo = dot(place, arrived[0, :steps])
    hi = dot(place, arrived[0, steps:])
    extra = dot(place, jnp.where(lax.rem(t // 2, 2) == 0, arrived[1, :steps], arrived[1, steps:]))
    extra = jnp.where(lax.rem(t, 2) == 0, extra[:half], extra[half:])
    chunk[0] = (total[0] + lo[:half]).astype(BF16)
    chunk[1] = (total[1] + lo[half:]).astype(BF16)
    chunk[2] = (total[2] + hi[:half]).astype(BF16)
    chunk[3] = (total[3] + hi[half:]).astype(BF16)
    chunk[4] = (total[4] + extra).astype(BF16)

    def ag_copy(j, slot):
        return pltpu.make_async_remote_copy(
            chunk, gathered.at[slot], ag_send.at[j], ag_recv.at[slot],
            device_id=(g, j), device_id_type=MESH,
        )

    for j in peers:
        ag_copy(j, t).start()
    gathered[t] = chunk[...]
    for j in peers:
        ag_copy(j, j).wait_recv()
    for j in range(n_t):
        for k in range(2):
            for h in range(2):
                out[h * half : (h + 1) * half, (2 * j + k) * LANES : (2 * j + k + 1) * LANES] = (
                    gathered[j, 2 * k + h]
                )
        tile = 2 * n_t + j // 2
        h = j % 2
        out[h * half : (h + 1) * half, tile * LANES : (tile + 1) * LANES] = gathered[j, 4]

    ask_copy.wait_send()
    for j in peers:
        rs_copy(j, t).wait_send()
        ag_copy(j, t).wait_send()
    for j in range(n_t):
        mv_copy(up, j, t).wait_send()


def per_device(n_dp, n_t, cache_keys, cache_values, lengths, finished, migrations, queries,
               new_keys, new_values, out_weight):
    steps, slots, width = queries.shape
    cache = cache_keys.shape[1]
    features = out_weight.shape[1]
    heads = width // HD
    rows = steps * slots
    fresh = jnp.concatenate([new_keys, new_values], axis=2).reshape(rows, 2 * HD)
    vmem = pl.BlockSpec(memory_space=pltpu.VMEM)
    smem = pl.BlockSpec(memory_space=pltpu.SMEM)
    anywhere = pl.BlockSpec(memory_space=pl.ANY)
    dma = pltpu.SemaphoreType.DMA
    result = pl.pallas_call(
        functools.partial(kernel, slots=slots, steps=steps, heads=heads, n_dp=n_dp, n_t=n_t),
        out_shape=jax.ShapeDtypeStruct((rows, features), BF16),
        in_specs=[smem, smem, vmem, vmem, vmem, anywhere, anywhere, anywhere],
        out_specs=vmem,
        scratch_shapes=[
            pltpu.VMEM((slots, cache, HD), BF16),
            pltpu.VMEM((slots, cache, HD), BF16),
            pltpu.VMEM((width, features), BF16),
            pltpu.VMEM(((heads + 2) * steps, HD), BF16),
            pltpu.VMEM(((heads + 2) * steps, HD), BF16),
            pltpu.VMEM((n_t, 5, rows // 2, LANES), BF16),
            pltpu.VMEM((n_t, 5, rows // 2, LANES), BF16),
            pltpu.VMEM((n_t, 2, 2 * steps, LANES), BF16),
            pltpu.VMEM((n_t, 2, 2 * steps, LANES), BF16),
            pltpu.VMEM((5, rows // 2, LANES), BF16),
            pltpu.VMEM((n_t, 5, rows // 2, LANES), BF16),
            dma((3,)), dma, dma, dma((n_t,)), dma((n_t,)), dma((n_t,)), dma((n_t,)),
            dma((n_t,)), dma((n_t,)),
        ],
        compiler_params=pltpu.CompilerParams(
            collective_id=0, has_side_effects=True, vmem_limit_bytes=48 << 20
        ),
    )(
        lengths, finished, migrations.T, queries.reshape(rows, width), fresh,
        cache_keys, cache_values, out_weight,
    )
    return result.reshape(steps, slots, features)


def solution(mesh):
    sizes = dict(zip(mesh.axis_names, mesh.devices.shape))
    return jax.shard_map(
        functools.partial(per_device, sizes["dp"], sizes["tensor"]),
        mesh=mesh,
        in_specs=(
            P("dp", None, "tensor"),
            P("dp", None, "tensor"),
            P("dp"),
            P("dp"),
            P(),
            P(None, "dp", "tensor"),
            P(None, "dp", "tensor"),
            P(None, "dp", "tensor"),
            P("tensor", None),
        ),
        out_specs=P(None, "dp", None),
        check_vma=False,
    )
```

time: 135 us -> 59.4 us (0.44)
  the two profiles are of different devices: /device:TPU:32 before, /device:TPU:64 now
where the time goes in v1:
time: 59.4 us; the launch traced here: 59.1 us
  Pallas kernels  52 us (88%)
  local copies, waits for them, and re-layouts  6.39 us (11%)
  other arithmetic  0.72 us (1%)
    pallas_call x1, Pallas kernels, per_device(): pl.pallas_call(functools.partial(kernel, slots=slots, steps=steps, heads=...  52 us
    unnamed x10, local copies, waits for them, and re-layouts  4.8 us

profile of v1, /device:TPU:64, one launch (start us, length us, event | category | flops | bytes accessed | tf_op | source)
XLA Modules:
  0.0 59.1 jit_solution(9617374937399289475)
XLA Ops:
  0.0 0.7 %pad_maximum_fusion = bf16[8,4,256]{2,1,0:T(4,128)(2,1)S(1)} fusion(bf16[8,4,128]{2,1,0:T(4,128)(2,1)} %param.16, bf16[8,4,128]{2,1,0:T(4,128)(2,1)} %param.15), kind=kLoop, calls=%fused_computation | loop fusion | flops 32768 | bytes 32768 | tf_op jit(solution)/shard_map/concatenate | solution.py:242
  0.7 0.9 %reshape.9.query = bf16[32,1024]{1,0:T(8,128)(2,1)S(1)} reshape(bf16[8,4,1024]{2,1,0:T(4,128)(2,1)} %param.14) | data formatting | bytes 131072 | tf_op jit(solution)/shard_map/reshape | solution.py:271
  1.6 0.0 copy-start
  1.6 1.4 %copy-done = bf16[4,1536,128]{2,1,0:T(8,128)(2,1)S(1)} copy-done((bf16[4,1536,128]{2,1,0:T(8,128)(2,1)S(1)}, bf16[4,1536,128]{2,1,0:T(8,128)(2,1)}, u32[]{:S(2)}) %copy-start) | copy-done | bytes 1572888
  3.0 0.0 copy-start.1
  3.0 1.4 %copy-done.1 = bf16[4,1536,128]{2,1,0:T(8,128)(2,1)S(1)} copy-done((bf16[4,1536,128]{2,1,0:T(8,128)(2,1)S(1)}, bf16[4,1536,128]{2,1,0:T(8,128)(2,1)}, u32[]{:S(2)}) %copy-start.1) | copy-done | bytes 1572888
  4.4 0.0 copy-start.2
  4.4 0.7 %copy-done.2 = s32[64,4]{0,1:T(4,128)S(1)} copy-done((s32[64,4]{0,1:T(4,128)S(1)}, s32[64,4]{0,1:T(4,128)}, u32[]{:S(2)}) %copy-start.2) | copy-done | bytes 1048
  5.1 0.0 copy-start.3
  5.1 0.7 %copy-done.3 = s32[4]{0:T(128)S(1)} copy-done((s32[4]{0:T(128)S(1)}, s32[4]{0:T(128)}, u32[]{:S(2)}) %copy-start.3) | copy-done | bytes 40
  5.8 0.0 copy-start.4
  5.8 0.7 %copy-done.4 = s32[4]{0:T(128)S(1)} copy-done((s32[4]{0:T(128)S(1)}, s32[4]{0:T(128)}, u32[]{:S(2)}) %copy-start.4) | copy-done | bytes 40
  6.4 52.0 %shard_map.91 = bf16[32,2560]{1,0:T(8,128)(2,1)S(1)} custom-call(s32[4]{0:T(128)S(1)} %copy-done.3, s32[4]{0:T(128)S(1)} %copy-done.4, s32[4,64]{1,0:T(4,128)S(1)} %bitcast.1, bf16[32,1024]{1,0:T(8,128)(2,1)S(1)} %reshape.9.query, bf16[32,256]{1,0:T(8,128)(2,1)S(1)} %reshape.10.fresh, bf16[4,1536,128]{2,1,0:T(8,128)(2,1)S(1)} %copy-done, ...), custom_call_target="tpu_custom_call" | custom-call | tf_op jit(solution)/shard_map/pallas_call | solution.py:247
  58.4 0.7 %reshape.11 = bf16[8,4,2560]{2,1,0:T(4,128)(2,1)} reshape(bf16[32,2560]{1,0:T(8,128)(2,1)S(1)} %shard_map.91) | data formatting | bytes 327680 | tf_op jit(solution)/shard_map/reshape | solution.py:274
  (1 shorter events, 0.0 us)
Async XLA Ops:
  1.6 1.4 %copy-start = (bf16[4,1536,128]{2,1,0:T(8,128)(2,1)S(1)}, bf16[4,1536,128]{2,1,0:T(8,128)(2,1)}, u32[]{:S(2)}) copy-start(bf16[4,1536,128]{2,1,0:T(8,128)(2,1)} %keys_hbm.1) | copy-start | bytes 4718596
  3.0 1.4 %copy-start.1 = (bf16[4,1536,128]{2,1,0:T(8,128)(2,1)S(1)}, bf16[4,1536,128]{2,1,0:T(8,128)(2,1)}, u32[]{:S(2)}) copy-start(bf16[4,1536,128]{2,1,0:T(8,128)(2,1)} %values_hbm.1) | copy-start | bytes 4718596
  4.4 0.7 %copy-start.2 = (s32[64,4]{0,1:T(4,128)S(1)}, s32[64,4]{0,1:T(4,128)}, u32[]{:S(2)}) copy-start(s32[64,4]{0,1:T(4,128)} %param.13) | copy-start | bytes 3076
  5.1 0.7 %copy-start.3 = (s32[4]{0:T(128)S(1)}, s32[4]{0:T(128)}, u32[]{:S(2)}) copy-start(s32[4]{0:T(128)} %lengths.1) | copy-start | bytes 52
  5.8 0.7 %copy-start.4 = (s32[4]{0:T(128)S(1)}, s32[4]{0:T(128)}, u32[]{:S(2)}) copy-start(s32[4]{0:T(128)} %finished.1) | copy-start | bytes 52

commit v2 on v1

v2 whole, which is shorter than its diff:
```python
import functools

import jax
import jax.numpy as jnp
from jax import lax
from jax.experimental import pallas as pl
from jax.experimental.pallas import tpu as pltpu
from jax.sharding import PartitionSpec as P

HD = 128
BLOCK = 512
LANES = 128
MESH = pl.DeviceIdType.MESH
F32 = jnp.float32
BF16 = jnp.bfloat16


def one_hot(mask):
    return jnp.where(mask, 1.0, 0.0).astype(BF16)


def grid_ids(shape):
    return (
        lax.broadcasted_iota(jnp.int32, shape, 0),
        lax.broadcasted_iota(jnp.int32, shape, 1),
    )


def dot(a, b):
    return lax.dot_general(a, b, (((1,), (0,)), ((), ())), preferred_element_type=F32)


def dot_t(a, b):
    return lax.dot_general(a, b, (((1,), (1,)), ((), ())), preferred_element_type=F32)


def stack_heads(rows, heads):
    return jnp.concatenate([rows[:, h * HD : (h + 1) * HD] for h in range(heads)], axis=0)


def attend(query, keys, values, fresh_keys, fresh_values, limit, steps, heads):
    scale = 1.0 / HD**0.5
    scores = dot_t(query, keys) * scale
    fresh = dot_t(query, fresh_keys) * scale
    _, position = grid_ids(scores.shape)
    scores = jnp.where(position < limit, scores, -1e30)
    row, token = grid_ids(fresh.shape)
    fresh = jnp.where(token <= lax.rem(row, steps), fresh, -1e30)
    peak = jnp.maximum(
        jnp.max(scores, axis=1, keepdims=True), jnp.max(fresh, axis=1, keepdims=True)
    )
    weights = jnp.exp(scores - peak)
    fresh_weights = jnp.exp(fresh - peak)
    total = jnp.sum(weights, axis=1, keepdims=True) + jnp.sum(fresh_weights, axis=1, keepdims=True)
    mixed = dot(weights.astype(BF16), values) + dot(fresh_weights.astype(BF16), fresh_values)
    mixed = mixed / total
    return jnp.concatenate([mixed[h * steps : (h + 1) * steps] for h in range(heads)], axis=1)


def kernel(
    lengths_hbm, finished_hbm, mig_hbm, query_hbm, new_keys_hbm, new_values_hbm,
    keys_hbm, values_hbm, weight_hbm,
    out,
    lengths, finished, mig, query, new_keys, new_values, keys, values, weight,
    ask, asked, relay, part, reduced, moved_part, moved_in, total, chunk, gathered,
    load_sem, ask_send, ask_recv, relay_send, relay_recv,
    rs_send, rs_recv, mv_send, mv_recv, ag_send, ag_recv, ready, open_sem,
    *, slots, steps, heads, n_dp, n_t, parity,
):
    g, t = lax.axis_index("dp"), lax.axis_index("tensor")
    up, down = lax.rem(g + 1, n_dp), lax.rem(g + n_dp - 1, n_dp)
    rows = slots * steps
    is_src = lax.rem(g, 2) == parity
    is_dst = jnp.logical_not(is_src)
    late_dst = jnp.logical_and(lax.rem(g, 16) == 0, is_dst)
    late_src = jnp.logical_and(lax.rem(g, 16) == 15, is_src)
    relays = jnp.logical_and(jnp.logical_and(lax.rem(g, 16) == 7, is_src), t == 0)
    relay_group = lax.rem(g + n_dp - 9, n_dp)
    relay_dst = lax.rem(g + 9, n_dp)
    relay_src = lax.rem(g + 8, n_dp)
    late = parity == 1

    loads = [
        pltpu.make_async_copy(src, dst, load_sem.at[i])
        for i, (src, dst) in enumerate(
            [
                (mig_hbm, mig), (query_hbm, query), (new_keys_hbm, new_keys),
                (new_values_hbm, new_values), (lengths_hbm, lengths),
                (finished_hbm, finished), (keys_hbm, keys), (values_hbm, values),
                (weight_hbm, weight),
            ]
        )
    ]
    for load in loads:
        load.start()

    barrier = pltpu.get_barrier_semaphore()

    def greet(group, other):
        pl.semaphore_signal(barrier, inc=1, device_id=(group, other), device_id_type=MESH)

    for j in range(n_t):

        @pl.when(t != j)
        def _():
            greet(g, j)

    if late:

        @pl.when(jnp.logical_and(is_src, jnp.logical_not(late_src)))
        def _():
            for j in range(n_t):
                greet(up, j)

        @pl.when(late_dst)
        def _():
            for j in range(n_t):
                greet(down, j)

        @pl.when(relays)
        def _():
            for j in range(n_t):
                greet(relay_dst, j)
                greet(relay_src, j)

    else:

        @pl.when(is_src)
        def _():
            for j in range(n_t):
                greet(up, j)

    for load in loads[:6]:
        load.wait()
    sending = mig[0:1, :] == g
    arriving = mig[1:2, :] == g
    has_send = jnp.sum(sending.astype(jnp.int32)) > 0
    has_arrival = jnp.sum(arriving.astype(jnp.int32)) > 0
    sent_row = jnp.sum(jnp.where(sending, mig[2:3, :], 0))
    arrival_slot = jnp.sum(jnp.where(arriving, mig[3:4, :], 0))

    def flat(ref):
        return jnp.concatenate([ref[s].astype(F32) for s in range(steps)], axis=0)

    i, j = grid_ids((rows + steps, rows))
    slot = jnp.where(i < rows, i // steps, arrival_slot)
    order = one_hot(j == lax.rem(i, steps) * slots + slot)
    by_slot = dot(order, flat(query).astype(BF16))
    fresh = jnp.concatenate([flat(new_keys), flat(new_values)], axis=1).astype(BF16)
    fresh_by_slot = dot(order, fresh)
    ask[0 : heads * steps, :] = stack_heads(by_slot[rows:], heads).astype(BF16)
    ask[heads * steps :, :] = stack_heads(fresh_by_slot[rows:], 2).astype(BF16)

    zeros = jnp.zeros((16 - steps, HD), F32)

    def pad(x):
        return jnp.concatenate([x, zeros], axis=0).astype(BF16)

    loads[6].wait()
    loads[7].wait()
    attended = []
    for r in range(slots):
        mine = slice(r * steps, (r + 1) * steps)
        mixed = attend(
            stack_heads(by_slot[mine], heads).astype(BF16),
            keys[r], values[r],
            pad(fresh_by_slot[mine, :HD]), pad(fresh_by_slot[mine, HD:]),
            lengths[r] * BLOCK, steps, heads,
        )
        stays = jnp.logical_and(
            finished[r] == 0, jnp.logical_not(jnp.logical_and(has_send, sent_row == r))
        )
        attended.append(jnp.where(stays, mixed, 0.0))
    attended = jnp.concatenate(attended, axis=0).astype(BF16)
    i, j = grid_ids((rows, rows))
    to_steps = one_hot(j == lax.rem(i, slots) * steps + i // slots)
    attended = dot(to_steps, attended).astype(BF16)

    loads[8].wait()
    half = rows // 2
    for c in range(10):
        block = dot(attended, weight[:, 256 * c : 256 * (c + 1)]).astype(BF16)
        for k in range(2):
            for h in range(2):
                piece = block[h * half : (h + 1) * half, k * LANES : (k + 1) * LANES]
                if c < 8:
                    part[c, 2 * k + h] = piece
                else:
                    part[2 * (2 * (c - 8) + k) + h, 4] = piece

    if late:
        greeted = (n_t - 1) + jnp.where(
            is_src, jnp.where(late_src, n_t + 1, 0), jnp.where(late_dst, 1, n_t)
        )
    else:
        greeted = (n_t - 1) + jnp.where(is_src, 0, n_t)
    pl.semaphore_wait(barrier, greeted)

    def ask_copy(group, other):
        return pltpu.make_async_remote_copy(
            ask, asked, ask_send, ask_recv, device_id=(group, other), device_id_type=MESH
        )

    def relay_copy(slot, group):
        return pltpu.make_async_remote_copy(
            ask, relay.at[slot], ask_send, relay_recv.at[slot],
            device_id=(group, 0), device_id_type=MESH,
        )

    def pass_copy(j):
        return pltpu.make_async_remote_copy(
            relay.at[j], asked, relay_send.at[j], ask_recv,
            device_id=(relay_src, j), device_id_type=MESH,
        )

    def rs_copy(j, slot):
        return pltpu.make_async_remote_copy(
            part.at[j], reduced.at[slot], rs_send.at[j], rs_recv.at[slot],
            device_id=(g, j), device_id_type=MESH,
        )

    def mv_copy(j, slot):
        return pltpu.make_async_remote_copy(
            moved_part.at[j], moved_in.at[slot], mv_send.at[j], mv_recv.at[slot],
            device_id=(up, j), device_id_type=MESH,
        )

    def ag_copy(j, slot):
        return pltpu.make_async_remote_copy(
            chunk, gathered.at[slot], ag_send.at[j], ag_recv.at[slot],
            device_id=(g, j), device_id_type=MESH,
        )

    def tell(sem, group, j):
        pl.semaphore_signal(sem, inc=1, device_id=(group, j), device_id_type=MESH)

    if late:

        @pl.when(late_dst)
        def _():
            relay_copy(t, relay_group).start()

        @pl.when(late_src)
        def _():
            tell(open_sem, lax.rem(g + n_dp - 8, n_dp), 0)

        @pl.when(jnp.logical_and(is_dst, jnp.logical_not(late_dst)))
        def _():
            ask_copy(down, t).start()
            for j in range(n_t):
                tell(ready, down, j)

    else:

        @pl.when(is_dst)
        def _():
            ask_copy(down, t).start()
            for j in range(n_t):
                tell(ready, down, j)

    for j in reversed(range(n_t)):

        @pl.when(t != j)
        def _():
            rs_copy(j, t).start()

    if late:

        @pl.when(relays)
        def _():
            pl.semaphore_wait(open_sem, n_t)
            for j in reversed(range(n_t)):
                relay_copy(j, g).wait_recv()
                pass_copy(j).start()

    @pl.when(is_src)
    def _():
        ask_copy(g, t).wait_recv()
        asked_fresh = asked[heads * steps :, :].astype(F32)
        moved = attend(
            asked[0 : heads * steps, :],
            keys[sent_row], values[sent_row],
            pad(asked_fresh[:steps]), pad(asked_fresh[steps:]),
            lengths[sent_row] * BLOCK, steps, heads,
        )
        moved = jnp.where(has_send, moved, 0.0).astype(BF16)
        for c in range(10):
            block = dot(moved, weight[:, 256 * c : 256 * (c + 1)])
            piece = jnp.concatenate([block[:, :LANES], block[:, LANES:]], axis=0).astype(BF16)
            if c < 8:
                moved_part[c, 0] = piece
            else:
                for j in range(4):
                    moved_part[4 * (c - 8) + j, 1] = piece
        if late:

            @pl.when(jnp.logical_not(late_src))
            def _():
                pl.semaphore_wait(ready, n_t)

        else:
            pl.semaphore_wait(ready, n_t)
        for j in reversed(range(n_t)):
            mv_copy(j, t).start()

    reduced[t] = part[t]
    for j in range(n_t):

        @pl.when(t != j)
        def _():
            rs_copy(j, j).wait_recv()

    acc = reduced[0].astype(F32)
    for j in range(1, n_t):
        acc = acc + reduced[j].astype(F32)
    total[...] = acc

    @pl.when(is_dst)
    def _():
        for j in range(n_t):
            mv_copy(j, j).wait_recv()
        arrived = moved_in[0].astype(F32)
        for j in range(1, n_t):
            arrived = arrived + moved_in[j].astype(F32)
        arrived = jnp.where(has_arrival, arrived, 0.0).astype(BF16)
        i, j = grid_ids((rows, steps))
        place = one_hot(jnp.logical_and(lax.rem(i, slots) == arrival_slot, i // slots == j))
        lo = dot(place, arrived[0, :steps])
        hi = dot(place, arrived[0, steps:])
        extra = dot(
            place, jnp.where(lax.rem(t // 2, 2) == 0, arrived[1, :steps], arrived[1, steps:])
        )
        extra = jnp.where(lax.rem(t, 2) == 0, extra[:half], extra[half:])
        total[0] += lo[:half]
        total[1] += lo[half:]
        total[2] += hi[:half]
        total[3] += hi[half:]
        total[4] += extra

    chunk[...] = total[...].astype(BF16)
    for j in range(n_t):

        @pl.when(t != j)
        def _():
            ag_copy(j, t).start()

    gathered[t] = chunk[...]
    for j in range(n_t):

        @pl.when(t != j)
        def _():
            ag_copy(j, j).wait_recv()

    for j in range(n_t):
        for k in range(2):
            for h in range(2):
                out[h * half : (h + 1) * half, (2 * j + k) * LANES : (2 * j + k + 1) * LANES] = (
                    gathered[j, 2 * k + h]
                )
        tile = 2 * n_t + j // 2
        h = j % 2
        out[h * half : (h + 1) * half, tile * LANES : (tile + 1) * LANES] = gathered[j, 4]

    for j in range(n_t):

        @pl.when(t != j)
        def _():
            rs_copy(j, t).wait_send()
            ag_copy(j, t).wait_send()

    @pl.when(is_src)
    def _():
        for j in range(n_t):
            mv_copy(j, t).wait_send()

    @pl.when(is_dst)
    def _():
        ask_copy(down, t).wait_send()

    if late:

        @pl.when(relays)
        def _():
            for j in range(n_t):
                pass_copy(j).wait_send()


def parity_kernel(mig_hbm, out, mig, sem):
    load = pltpu.make_async_copy(mig_hbm, mig, sem)
    load.start()
    load.wait()
    out[0] = lax.rem(mig[0, 0], 2)


def source_parity(moves):
    return pl.pallas_call(
        parity_kernel,
        out_shape=jax.ShapeDtypeStruct((1,), jnp.int32),
        in_specs=[pl.BlockSpec(memory_space=pltpu.HBM)],
        out_specs=pl.BlockSpec(memory_space=pltpu.SMEM),
        scratch_shapes=[pltpu.SMEM(moves.shape, jnp.int32), pltpu.SemaphoreType.DMA],
    )(moves)[0]


def project(parity, n_dp, n_t, *operands):
    lengths, finished, moves, queries, new_keys, new_values, keys, values, weight = operands
    steps, slots, width = queries.shape
    features = weight.shape[1]
    heads = width // HD
    rows = steps * slots
    dma = pltpu.SemaphoreType.DMA
    regular = pltpu.SemaphoreType.REGULAR
    asks = ((heads + 2) * steps, HD)
    pieces = (n_t, 5, rows // 2, LANES)
    moved = (n_t, 2, 2 * steps, LANES)
    return pl.pallas_call(
        functools.partial(
            kernel, slots=slots, steps=steps, heads=heads, n_dp=n_dp, n_t=n_t, parity=parity
        ),
        out_shape=jax.ShapeDtypeStruct((rows, features), BF16),
        in_specs=[pl.BlockSpec(memory_space=pltpu.HBM)] * 9,
        out_specs=pl.BlockSpec(memory_space=pltpu.VMEM),
        scratch_shapes=[
            pltpu.SMEM(lengths.shape, jnp.int32),
            pltpu.SMEM(finished.shape, jnp.int32),
            pltpu.VMEM(moves.shape, jnp.int32),
            pltpu.VMEM(queries.shape, BF16),
            pltpu.VMEM(new_keys.shape, BF16),
            pltpu.VMEM(new_values.shape, BF16),
            pltpu.VMEM(keys.shape, BF16),
            pltpu.VMEM(values.shape, BF16),
            pltpu.VMEM(weight.shape, BF16),
            pltpu.VMEM(asks, BF16),
            pltpu.VMEM(asks, BF16),
            pltpu.VMEM((n_t,) + asks, BF16),
            pltpu.VMEM(pieces, BF16),
            pltpu.VMEM(pieces, BF16),
            pltpu.VMEM(moved, BF16),
            pltpu.VMEM(moved, BF16),
            pltpu.VMEM(pieces[1:], F32),
            pltpu.VMEM(pieces[1:], BF16),
            pltpu.VMEM(pieces, BF16),
            dma((9,)), dma, dma, dma((n_t,)), dma((n_t,)),
            dma((n_t,)), dma((n_t,)), dma((n_t,)), dma((n_t,)), dma((n_t,)), dma((n_t,)),
            regular, regular,
        ],
        compiler_params=pltpu.CompilerParams(
            collective_id=parity, has_side_effects=True, vmem_limit_bytes=48 << 20
        ),
    )(*operands)


def per_device(n_dp, n_t, cache_keys, cache_values, lengths, finished, migrations, queries,
               new_keys, new_values, out_weight):
    steps, slots, _ = queries.shape
    moves = migrations.T
    result = lax.cond(
        source_parity(moves) == 0,
        functools.partial(project, 0, n_dp, n_t),
        functools.partial(project, 1, n_dp, n_t),
        lengths, finished, moves, queries, new_keys, new_values,
        cache_keys, cache_values, out_weight,
    )
    return result.reshape(steps, slots, out_weight.shape[1])


def solution(mesh):
    sizes = dict(zip(mesh.axis_names, mesh.devices.shape))
    return jax.shard_map(
        functools.partial(per_device, sizes["dp"], sizes["tensor"]),
        mesh=mesh,
        in_specs=(
            P("dp", None, "tensor"),
            P("dp", None, "tensor"),
            P("dp"),
            P("dp"),
            P(),
            P(None, "dp", "tensor"),
            P(None, "dp", "tensor"),
            P(None, "dp", "tensor"),
            P("tensor", None),
        ),
        out_specs=P(None, "dp", None),
        check_vma=False,
    )
```

time: 59.4 us -> 39 us (0.66)
  the two profiles are of different devices: /device:TPU:64 before, /device:TPU:1 now
where the time goes in v2:
time: 39 us; the launch traced here: 38.8 us
  Pallas kernels  37.4 us (96%)
  local copies, waits for them, and re-layouts  0.71 us (2%)
  between operations  0.67 us (2%)
    pallas_call x1, Pallas kernels, project(): pl.pallas_call(functools.partial(kernel, slots=slots, steps=steps, heads=...  36.2 us
    pallas_call x1, Pallas kernels, source_parity(): pl.pallas_call(parity_kernel, out_shape=jax.ShapeDtypeStruct((1,), jnp.in...  1.22 us

profile of v2, /device:TPU:1, one launch (start us, length us, event | category | flops | bytes accessed | tf_op | source)
XLA Modules:
  0.0 38.8 jit_solution(12227078743840321907)
XLA Ops:
  0.0 1.2 %shard_map.93 = s32[1]{0:T(128)} custom-call(s32[4,64]{1,0:T(4,128)} %bitcast.2), custom_call_target="tpu_custom_call" | custom-call | tf_op jit(solution)/shard_map/pallas_call | solution.py:396
  1.9 36.3 %conditional.1 = (bf16[8,4,2560]{2,1,0:T(4,128)(2,1)S(1)}) conditional(s32[]{:T(128)} %bitcast.1, (s32[4]{0:T(128)}, s32[4]{0:T(128)}, s32[4,64]{1,0:T(4,128)}, bf16[8,4,1024]{2,1,0:T(4,128)(2,1)}, bf16[8,4,128]{2,1,0:T(4,128)(2,1)}, /*index=5*/bf16[8,4,128]{2,1,0:T(4,128)(2,1)}, bf16[4,1536,128]{2,1,0:T(8,128)(2,1)}, ...), branch_computations={%region_0.0_spmd, %region_1.0_spmd} | conditional | bytes 327688 | solution.py:457
  1.9 36.2 %branch_1_fun.1 = bf16[32,2560]{1,0:T(8,128)(2,1)S(1)} custom-call(s32[4]{0:T(128)} %get-tuple-element.54.lengths_hbm, s32[4]{0:T(128)} %get-tuple-element.55.finished_hbm, s32[4,64]{1,0:T(4,128)} %get-tuple-element.56.mig_hbm, bf16[8,4,1024]{2,1,0:T(4,128)(2,1)} %get-tuple-element.57.query_hbm, bf16[8,4,128]{2,1,0:T(4,128)(2,1)} %get-tuple-element.58.new_keys_hbm, ...), custom_call_target="tpu_custom_call" | custom-call | tf_op jit(solution)/shard_map/cond/branch_1_fun/pallas_call | solution.py:416
  38.1 0.0 copy-start
  38.1 0.7 %copy-done = bf16[8,4,2560]{2,1,0:T(4,128)(2,1)} copy-done((bf16[8,4,2560]{2,1,0:T(4,128)(2,1)}, bf16[8,4,2560]{2,1,0:T(4,128)(2,1)S(1)}, u32[]{:S(2)}) %copy-start) | copy-done | bytes 163864
  (1 shorter events, 0.0 us)
Async XLA Ops:
  38.1 0.7 %copy-start = (bf16[8,4,2560]{2,1,0:T(4,128)(2,1)}, bf16[8,4,2560]{2,1,0:T(4,128)(2,1)S(1)}, u32[]{:S(2)}) copy-start(bf16[8,4,2560]{2,1,0:T(4,128)(2,1)S(1)} %get-tuple-element.66) | copy-start | bytes 491524

commit v3 on v2

--- a/solution.py
+++ b/solution.py
@@ -64,7 +64,7 @@
     lengths, finished, mig, query, new_keys, new_values, keys, values, weight,
     ask, asked, relay, part, reduced, moved_part, moved_in, total, chunk, gathered,
     load_sem, ask_send, ask_recv, relay_send, relay_recv,
-    rs_send, rs_recv, mv_send, mv_recv, ag_send, ag_recv, ready, open_sem,
+    rs_send, rs_recv, mv_send, mv_recv, ag_send, ag_recv, here, ready, open_sem,
     *, slots, steps, heads, n_dp, n_t, parity,
 ):
     g, t = lax.axis_index("dp"), lax.axis_index("tensor")
@@ -72,63 +72,174 @@
     rows = slots * steps
     is_src = lax.rem(g, 2) == parity
     is_dst = jnp.logical_not(is_src)
-    late_dst = jnp.logical_and(lax.rem(g, 16) == 0, is_dst)
-    late_src = jnp.logical_and(lax.rem(g, 16) == 15, is_src)
-    relays = jnp.logical_and(jnp.logical_and(lax.rem(g, 16) == 7, is_src), t == 0)
-    relay_group = lax.rem(g + n_dp - 9, n_dp)
+    far = parity == 1
+    place16 = lax.rem(g, 16)
+    far_src_first = jnp.logical_and(is_src, place16 == 7)
+    far_dst_last = jnp.logical_and(is_dst, place16 == 8)
+    far_src_last = jnp.logical_and(is_src, place16 == 15)
+    far_dst_first = jnp.logical_and(is_dst, place16 == 0)
+    near = jnp.logical_or(
+        jnp.logical_and(is_src, jnp.logical_and(place16 != 7, place16 != 15)),
+        jnp.logical_and(is_dst, jnp.logical_and(place16 != 8, place16 != 0)),
+    )
+    relays = jnp.logical_and(far_src_first, t == 0)
+    relay_of_dst = lax.rem(g + n_dp - 9, n_dp)
+    relay_of_src = lax.rem(g + n_dp - 8, n_dp)
     relay_dst = lax.rem(g + 9, n_dp)
     relay_src = lax.rem(g + 8, n_dp)
-    late = parity == 1
-
+
+    def when(*conditions):
+        return pl.when(functools.reduce(jnp.logical_and, conditions))
+
+    pairs = [
+        (mig_hbm, mig), (query_hbm, query), (new_keys_hbm, new_keys),
+        (new_values_hbm, new_values), (lengths_hbm, lengths), (finished_hbm, finished),
+    ]
+    pairs += [(keys_hbm.at[r], keys.at[r]) for r in range(slots)]
+    pairs += [(values_hbm.at[r], values.at[r]) for r in range(slots)]
+    pairs += [
+        (weight_hbm.at[:, pl.ds(256 * c, 256)], weight.at[:, pl.ds(256 * c, 256)])
+        for c in range(10)
+    ]
     loads = [
-        pltpu.make_async_copy(src, dst, load_sem.at[i])
-        for i, (src, dst) in enumerate(
-            [
-                (mig_hbm, mig), (query_hbm, query), (new_keys_hbm, new_keys),
-                (new_values_hbm, new_values), (lengths_hbm, lengths),
-                (finished_hbm, finished), (keys_hbm, keys), (values_hbm, values),
-                (weight_hbm, weight),
-            ]
-        )
+        pltpu.make_async_copy(src, dst, load_sem.at[i]) for i, (src, dst) in enumerate(pairs)
     ]
     for load in loads:
         load.start()
+    key_loads, value_loads = loads[6 : 6 + slots], loads[6 + slots : 6 + 2 * slots]
+    weight_loads = loads[6 + 2 * slots :]
 
     barrier = pltpu.get_barrier_semaphore()
 
     def greet(group, other):
         pl.semaphore_signal(barrier, inc=1, device_id=(group, other), device_id_type=MESH)
 
+    def tell(sem, group, other):
+        pl.semaphore_signal(sem, inc=1, device_id=(group, other), device_id_type=MESH)
+
+    near_src = jnp.logical_and(is_src, near) if far else is_src
+    near_dst = jnp.logical_and(is_dst, near) if far else is_dst
+
+    def rank_of(group, other):
+        return jnp.where(jnp.logical_and(group == 0, other == 0), n_t, other)
+
+    rank = rank_of(g, t)
+    last = rank == n_t
+    before_last = jnp.logical_and(g == 0, t > 0)
+
     for j in range(n_t):
 
-        @pl.when(t != j)
+        @when(rank_of(g, j) > rank)
         def _():
             greet(g, j)
 
-    if late:
-
-        @pl.when(jnp.logical_and(is_src, jnp.logical_not(late_src)))
+        @when(near_src, j >= rank)
+        def _():
+            greet(up, j)
+
+        @when(near_dst, rank_of(down, j) >= t)
+        def _():
+            greet(down, j)
+
+    if far:
+
+        @when(far_src_first)
         def _():
             for j in range(n_t):
                 greet(up, j)
 
-        @pl.when(late_dst)
+        @when(far_dst_first, jnp.logical_not(last))
         def _():
             for j in range(n_t):
                 greet(down, j)
 
-        @pl.when(relays)
+        @when(relays)
         def _():
             for j in range(n_t):
                 greet(relay_dst, j)
                 greet(relay_src, j)
 
+        greeted = jnp.where(
+            near, t + 1,
+            jnp.where(
+                far_dst_last, n_t,
+                jnp.where(far_src_last, n_t + 1, jnp.where(far_dst_first, 1, 0)),
+            ),
+        )
+        greeted = jnp.where(last, n_t, t + greeted)
+        fewer = jnp.logical_or(before_last, g == n_dp - 1)
     else:
-
-        @pl.when(is_src)
+        greeted = jnp.where(last, 2 * n_t - 1, 2 * t + 1)
+        fewer = jnp.logical_or(before_last, g == 1)
+    greeted = greeted - jnp.where(fewer, 1, 0)
+
+    @when(greeted > 0)
+    def _():
+        pl.semaphore_wait(barrier, greeted)
+
+
+    for j in range(n_t):
+
+        @when(rank_of(g, j) < rank)
+        def _():
+            tell(here.at[t], g, j)
+
+        @when(near_dst, rank_of(down, j) < t)
+        def _():
+            tell(ready.at[t], down, j)
+
+    ask_later = jnp.logical_and(g == 1, t == 0)
+    if far:
+
+        @when(far_dst_last)
         def _():
             for j in range(n_t):
-                greet(up, j)
+                tell(ready.at[t], down, j)
+
+        @when(far_src_last)
+        def _():
+            tell(open_sem.at[t], relay_of_src, 0)
+
+    else:
+
+        @when(last)
+        def _():
+            tell(ready.at[0], up, 0)
+
+    def ask_copy(group, other):
+        return pltpu.make_async_remote_copy(
+            ask, asked, ask_send, ask_recv, device_id=(group, other), device_id_type=MESH
+        )
+
+    def relay_copy(slot, group):
+        return pltpu.make_async_remote_copy(
+            ask, relay.at[slot], ask_send, relay_recv.at[slot],
+            device_id=(group, 0), device_id_type=MESH,
+        )
+
+    def pass_copy(j):
+        return pltpu.make_async_remote_copy(
+            relay.at[j], asked, relay_send.at[j], ask_recv,
+            device_id=(relay_src, j), device_id_type=MESH,
+        )
+
+    def rs_copy(j, slot):
+        return pltpu.make_async_remote_copy(
+            part.at[j], reduced.at[slot], rs_send.at[j], rs_recv.at[slot],
+            device_id=(g, j), device_id_type=MESH,
+        )
+
+    def mv_copy(j, slot):
+        return pltpu.make_async_remote_copy(
+            moved_part.at[j], moved_in.at[slot], mv_send.at[j], mv_recv.at[slot],
+            device_id=(up, j), device_id_type=MESH,
+        )
+
+    def ag_copy(j, slot):
+        return pltpu.make_async_remote_copy(
+            chunk, gathered.at[slot], ag_send.at[j], ag_recv.at[slot],
+            device_id=(g, j), device_id_type=MESH,
+        )
 
     for load in loads[:6]:
         load.wait()
@@ -151,15 +262,31 @@
     ask[0 : heads * steps, :] = stack_heads(by_slot[rows:], heads).astype(BF16)
     ask[heads * steps :, :] = stack_heads(fresh_by_slot[rows:], 2).astype(BF16)
 
+    if far:
+
+        @when(is_dst, jnp.logical_not(far_dst_first))
+        def _():
+            ask_copy(down, t).start()
+
+        @when(far_dst_first)
+        def _():
+            relay_copy(t, relay_of_dst).start()
+
+    else:
+
+        @when(is_dst, jnp.logical_not(ask_later))
+        def _():
+            ask_copy(down, t).start()
+
     zeros = jnp.zeros((16 - steps, HD), F32)
 
     def pad(x):
         return jnp.concatenate([x, zeros], axis=0).astype(BF16)
 
-    loads[6].wait()
-    loads[7].wait()
     attended = []
     for r in range(slots):
+        key_loads[r].wait()
+        value_loads[r].wait()
         mine = slice(r * steps, (r + 1) * steps)
         mixed = attend(
             stack_heads(by_slot[mine], heads).astype(BF16),
@@ -176,10 +303,10 @@
     to_steps = one_hot(j == lax.rem(i, slots) * steps + i // slots)
     attended = dot(to_steps, attended).astype(BF16)
 
-    loads[8].wait()
     half = rows // 2
-    for c in range(10):
-        block = dot(attended, weight[:, 256 * c : 256 * (c + 1)]).astype(BF16)
+
+    def put_part(c, block):
+        block = block.astype(BF16)
         for k in range(2):
             for h in range(2):
                 piece = block[h * half : (h + 1) * half, k * LANES : (k + 1) * LANES]
@@ -188,93 +315,18 @@
                 else:
                     part[2 * (2 * (c - 8) + k) + h, 4] = piece
 
-    if late:
-        greeted = (n_t - 1) + jnp.where(
-            is_src, jnp.where(late_src, n_t + 1, 0), jnp.where(late_dst, 1, n_t)
-        )
-    else:
-        greeted = (n_t - 1) + jnp.where(is_src, 0, n_t)
-    pl.semaphore_wait(barrier, greeted)
-
-    def ask_copy(group, other):
-        return pltpu.make_async_remote_copy(
-            ask, asked, ask_send, ask_recv, device_id=(group, other), device_id_type=MESH
-        )
-
-    def relay_copy(slot, group):
-        return pltpu.make_async_remote_copy(
-            ask, relay.at[slot], ask_send, relay_recv.at[slot],
-            device_id=(group, 0), device_id_type=MESH,
-        )
-
-    def pass_copy(j):
-        return pltpu.make_async_remote_copy(
-            relay.at[j], asked, relay_send.at[j], ask_recv,
-            device_id=(relay_src, j), device_id_type=MESH,
-        )
-
-    def rs_copy(j, slot):
-        return pltpu.make_async_remote_copy(
-            part.at[j], reduced.at[slot], rs_send.at[j], rs_recv.at[slot],
-            device_id=(g, j), device_id_type=MESH,
-        )
-
-    def mv_copy(j, slot):
-        return pltpu.make_async_remote_copy(
-            moved_part.at[j], moved_in.at[slot], mv_send.at[j], mv_recv.at[slot],
-            device_id=(up, j), device_id_type=MESH,
-        )
-
-    def ag_copy(j, slot):
-        return pltpu.make_async_remote_copy(
-            chunk, gathered.at[slot], ag_send.at[j], ag_recv.at[slot],
-            device_id=(g, j), device_id_type=MESH,
-        )
-
-    def tell(sem, group, j):
-        pl.semaphore_signal(sem, inc=1, device_id=(group, j), device_id_type=MESH)
-
-    if late:
-
-        @pl.when(late_dst)
-        def _():
-            relay_copy(t, relay_group).start()
-
-        @pl.when(late_src)
-        def _():
-            tell(open_sem, lax.rem(g + n_dp - 8, n_dp), 0)
-
-        @pl.when(jnp.logical_and(is_dst, jnp.logical_not(late_dst)))
-        def _():
-            ask_copy(down, t).start()
-            for j in range(n_t):
-                tell(ready, down, j)
-
-    else:
-
-        @pl.when(is_dst)
-        def _():
-            ask_copy(down, t).start()
-            for j in range(n_t):
-                tell(ready, down, j)
-
-    for j in reversed(range(n_t)):
-
-        @pl.when(t != j)
-        def _():
-            rs_copy(j, t).start()
-
-    if late:
-
-        @pl.when(relays)
-        def _():
-            pl.semaphore_wait(open_sem, n_t)
-            for j in reversed(range(n_t)):
-                relay_copy(j, g).wait_recv()
-                pass_copy(j).start()
-
-    @pl.when(is_src)
-    def _():
+    def put_moved(c, block):
+        piece = jnp.concatenate([block[:, :LANES], block[:, LANES:]], axis=0).astype(BF16)
+        if c < 8:
+            moved_part[c, 0] = piece
+        else:
+            for j in range(4):
+                moved_part[4 * (c - 8) + j, 1] = piece
+
+    def columns(c):
+        return weight[:, 256 * c : 256 * (c + 1)]
+
+    def attend_moved():
         ask_copy(g, t).wait_recv()
         asked_fresh = asked[heads * steps :, :].astype(F32)
         moved = attend(
@@ -283,25 +335,94 @@
             pad(asked_fresh[:steps]), pad(asked_fresh[steps:]),
             lengths[sent_row] * BLOCK, steps, heads,
         )
-        moved = jnp.where(has_send, moved, 0.0).astype(BF16)
+        return jnp.where(has_send, moved, 0.0).astype(BF16)
+
+    def send_all(parts, moved):
+        for j in reversed(range(n_t)):
+            if moved:
+
+                @when(near_src, j <= rank)
+                def _():
+                    mv_copy(j, t).start()
+
+            if parts:
+
+                @when(rank_of(g, j) < rank)
+                def _():
+                    rs_copy(j, t).start()
+
+        for j in list(range(1, n_t)) + [0]:
+            if moved:
+
+                @when(near_src, j > rank)
+                def _():
+                    pl.semaphore_wait(ready.at[j], 1)
+                    mv_copy(j, t).start()
+
+            if parts:
+
+                @when(rank_of(g, j) > rank)
+                def _():
+                    pl.semaphore_wait(here.at[j], 1)
+                    rs_copy(j, t).start()
+
+        if moved and far:
+
+            @when(far_src_first)
+            def _():
+                for j in range(n_t):
+                    pl.semaphore_wait(ready.at[j], 1)
+                    mv_copy(j, t).start()
+
+            @when(far_src_last)
+            def _():
+                for j in range(n_t):
+                    mv_copy(j, t).start()
+
+    if far:
         for c in range(10):
-            block = dot(moved, weight[:, 256 * c : 256 * (c + 1)])
-            piece = jnp.concatenate([block[:, :LANES], block[:, LANES:]], axis=0).astype(BF16)
-            if c < 8:
-                moved_part[c, 0] = piece
-            else:
-                for j in range(4):
-                    moved_part[4 * (c - 8) + j, 1] = piece
-        if late:
-
-            @pl.when(jnp.logical_not(late_src))
-            def _():
-                pl.semaphore_wait(ready, n_t)
-
-        else:
-            pl.semaphore_wait(ready, n_t)
-        for j in reversed(range(n_t)):
-            mv_copy(j, t).start()
+            weight_loads[c].wait()
+            put_part(c, dot(attended, columns(c)))
+        send_all(True, False)
+
+        @when(relays)
+        def _():
+            for j in range(n_t):
+                pl.semaphore_wait(open_sem.at[j], 1)
+                relay_copy(j, g).wait_recv()
+                pass_copy(j).start()
+
+        @when(is_src)
+        def _():
+            moved = attend_moved()
+            for c in range(10):
+                put_moved(c, dot(moved, columns(c)))
+            send_all(False, True)
+
+    else:
+
+        @when(is_src)
+        def _():
+            both = jnp.concatenate([attended.astype(F32), attend_moved().astype(F32)], axis=0)
+            both = both.astype(BF16)
+            for c in range(10):
+                weight_loads[c].wait()
+                block = dot(both, columns(c))
+                put_part(c, block[:rows])
+                put_moved(c, block[rows:])
+            send_all(True, True)
+
+        @when(ask_later)
+        def _():
+            pl.semaphore_wait(ready.at[0], 1)
+            ask_copy(down, t).start()
+
+        @when(is_dst)
+        def _():
+            for c in range(10):
+                weight_loads[c].wait()
+                put_part(c, dot(attended, columns(c)))
+            send_all(True, False)
 
     reduced[t] = part[t]
     for j in range(n_t):
@@ -377,7 +498,7 @@
     def _():
         ask_copy(down, t).wait_send()
 
-    if late:
+    if far:
 
         @pl.when(relays)
         def _():
@@ -440,9 +561,9 @@
             pltpu.VMEM(pieces[1:], F32),
             pltpu.VMEM(pieces[1:], BF16),
             pltpu.VMEM(pieces, BF16),
-            dma((9,)), dma, dma, dma((n_t,)), dma((n_t,)),
+            dma((6 + 2 * slots + 10,)), dma, dma, dma((n_t,)), dma((n_t,)),
             dma((n_t,)), dma((n_t,)), dma((n_t,)), dma((n_t,)), dma((n_t,)), dma((n_t,)),
-            regular, regular,
+            regular((n_t,)), regular((n_t,)), regular((n_t,)),
         ],
         compiler_params=pltpu.CompilerParams(
             collective_id=parity, has_side_effects=True, vmem_limit_bytes=48 << 20

time: 39 us -> 49.7 us (1.27)
  the two profiles are of different devices: /device:TPU:1 before, /device:TPU:32 now
where the time goes in v3:
time: 49.7 us; the launch traced here: 49.5 us
  Pallas kernels  48.1 us (97%)
  local copies, waits for them, and re-layouts  0.71 us (1%)
  between operations  0.67 us (1%)
    pallas_call x1, Pallas kernels, project(): pl.pallas_call(functools.partial(kernel, slots=slots, steps=steps, heads=...  46.9 us
    pallas_call x1, Pallas kernels, source_parity(): pl.pallas_call(parity_kernel, out_shape=jax.ShapeDtypeStruct((1,), jnp.in...  1.22 us

profile of v3, /device:TPU:32, one launch (start us, length us, event | category | flops | bytes accessed | tf_op | source)
XLA Modules:
  0.0 49.5 jit_solution(15232772490103349684)
XLA Ops:
  0.0 1.2 %shard_map.93 = s32[1]{0:T(128)} custom-call(s32[4,64]{1,0:T(4,128)} %bitcast.2), custom_call_target="tpu_custom_call" | custom-call | tf_op jit(solution)/shard_map/pallas_call | solution.py:517
  1.9 47.0 %conditional.1 = (bf16[8,4,2560]{2,1,0:T(4,128)(2,1)S(1)}) conditional(s32[]{:T(128)} %bitcast.1, (s32[4]{0:T(128)}, s32[4]{0:T(128)}, s32[4,64]{1,0:T(4,128)}, bf16[8,4,1024]{2,1,0:T(4,128)(2,1)}, bf16[8,4,128]{2,1,0:T(4,128)(2,1)}, /*index=5*/bf16[8,4,128]{2,1,0:T(4,128)(2,1)}, bf16[4,1536,128]{2,1,0:T(8,128)(2,1)}, ...), branch_computations={%region_0.0_spmd, %region_1.0_spmd} | conditional | bytes 327688 | solution.py:578
  1.9 46.9 %branch_0_fun.1 = bf16[32,2560]{1,0:T(8,128)(2,1)S(1)} custom-call(s32[4]{0:T(128)} %get-tuple-element.45.lengths_hbm, s32[4]{0:T(128)} %get-tuple-element.46.finished_hbm, s32[4,64]{1,0:T(4,128)} %get-tuple-element.47.mig_hbm, bf16[8,4,1024]{2,1,0:T(4,128)(2,1)} %get-tuple-element.48.query_hbm, bf16[8,4,128]{2,1,0:T(4,128)(2,1)} %get-tuple-element.49.new_keys_hbm, ...), custom_call_target="tpu_custom_call" | custom-call | tf_op jit(solution)/shard_map/cond/branch_0_fun/pallas_call | solution.py:537
  48.9 0.0 copy-start
  48.9 0.7 %copy-done = bf16[8,4,2560]{2,1,0:T(4,128)(2,1)} copy-done((bf16[8,4,2560]{2,1,0:T(4,128)(2,1)}, bf16[8,4,2560]{2,1,0:T(4,128)(2,1)S(1)}, u32[]{:S(2)}) %copy-start) | copy-done | bytes 163864
  (1 shorter events, 0.0 us)
Async XLA Ops:
  48.9 0.7 %copy-start = (bf16[8,4,2560]{2,1,0:T(4,128)(2,1)}, bf16[8,4,2560]{2,1,0:T(4,128)(2,1)S(1)}, u32[]{:S(2)}) copy-start(bf16[8,4,2560]{2,1,0:T(4,128)(2,1)S(1)} %get-tuple-element.66) | copy-start | bytes 491524

commit v4 on v3

--- a/solution.py
+++ b/solution.py
@@ -10,6 +10,7 @@
 HD = 128
 BLOCK = 512
 LANES = 128
+HELPER = 3
 MESH = pl.DeviceIdType.MESH
 F32 = jnp.float32
 BF16 = jnp.bfloat16
@@ -62,9 +63,11 @@
     keys_hbm, values_hbm, weight_hbm,
     out,
     lengths, finished, mig, query, new_keys, new_values, keys, values, weight,
-    ask, asked, relay, part, reduced, moved_part, moved_in, total, chunk, gathered,
+    ask, asked, relay, part, reduced, moved_part, moved_in, far_part, far_in, far_row, total, chunk,
+    gathered,
     load_sem, ask_send, ask_recv, relay_send, relay_recv,
-    rs_send, rs_recv, mv_send, mv_recv, ag_send, ag_recv, here, ready, open_sem,
+    rs_send, rs_recv, mv_send, mv_recv, ag_send, ag_recv, far_send, far_recv, row_send, row_recv,
+    here, ready, open_sem,
     *, slots, steps, heads, n_dp, n_t, parity,
 ):
     g, t = lax.axis_index("dp"), lax.axis_index("tensor")
@@ -83,6 +86,9 @@
         jnp.logical_and(is_dst, jnp.logical_and(place16 != 8, place16 != 0)),
     )
     relays = jnp.logical_and(far_src_first, t == 0)
+    owner = jnp.where(g == 0, 1, 0)
+    adds = jnp.logical_and(far_dst_first, t == owner)
+    owner_up = jnp.where(up == 0, 1, 0)
     relay_of_dst = lax.rem(g + n_dp - 9, n_dp)
     relay_of_src = lax.rem(g + n_dp - 8, n_dp)
     relay_dst = lax.rem(g + 9, n_dp)
@@ -148,7 +154,7 @@
             for j in range(n_t):
                 greet(up, j)
 
-        @when(far_dst_first, jnp.logical_not(last))
+        @when(adds)
         def _():
             for j in range(n_t):
                 greet(down, j)
@@ -163,11 +169,11 @@
             near, t + 1,
             jnp.where(
                 far_dst_last, n_t,
-                jnp.where(far_src_last, n_t + 1, jnp.where(far_dst_first, 1, 0)),
+                jnp.where(far_src_last, 2, jnp.where(far_dst_first, 1, 0)),
             ),
         )
         greeted = jnp.where(last, n_t, t + greeted)
-        fewer = jnp.logical_or(before_last, g == n_dp - 1)
+        fewer = before_last
     else:
         greeted = jnp.where(last, 2 * n_t - 1, 2 * t + 1)
         fewer = jnp.logical_or(before_last, g == 1)
@@ -184,14 +190,14 @@
         def _():
             tell(here.at[t], g, j)
 
-        @when(near_dst, rank_of(down, j) < t)
+        @when(near_dst, rank_of(down, j) < t, t != n_t - 1)
         def _():
             tell(ready.at[t], down, j)
 
     ask_later = jnp.logical_and(g == 1, t == 0)
     if far:
 
-        @when(far_dst_last)
+        @when(far_dst_last, t != n_t - 1)
         def _():
             for j in range(n_t):
                 tell(ready.at[t], down, j)
@@ -223,21 +229,42 @@
             device_id=(relay_src, j), device_id_type=MESH,
         )
 
-    def rs_copy(j, slot):
+    adder = list(range(n_t - 1)) + [HELPER]
+    side = [0] * (n_t - 1) + [1]
+
+    def rs_copy(c, slot):
         return pltpu.make_async_remote_copy(
-            part.at[j], reduced.at[slot], rs_send.at[j], rs_recv.at[slot],
-            device_id=(g, j), device_id_type=MESH,
-        )
-
-    def mv_copy(j, slot):
+            part.at[c], reduced.at[side[c], slot], rs_send.at[c], rs_recv.at[side[c], slot],
+            device_id=(g, adder[c]), device_id_type=MESH,
+        )
+
+    def mv_copy(c, slot):
         return pltpu.make_async_remote_copy(
-            moved_part.at[j], moved_in.at[slot], mv_send.at[j], mv_recv.at[slot],
-            device_id=(up, j), device_id_type=MESH,
-        )
-
-    def ag_copy(j, slot):
+            moved_part.at[c], moved_in.at[side[c], slot], mv_send.at[c],
+            mv_recv.at[side[c], slot], device_id=(up, adder[c]), device_id_type=MESH,
+        )
+
+    def far_copy(slot):
         return pltpu.make_async_remote_copy(
-            chunk, gathered.at[slot], ag_send.at[j], ag_recv.at[slot],
+            far_part, far_in.at[slot], far_send, far_recv.at[slot],
+            device_id=(up, owner_up), device_id_type=MESH,
+        )
+
+    tree = {0: (1, 2, 4), 2: (3,), 4: (5, 6), 6: (7,)}
+
+    def place_in_tree(j):
+        return jnp.where(j == owner, 0, jnp.where(j == 0, owner, j))
+
+    my_place = place_in_tree(t)
+
+    def row_copy(j):
+        return pltpu.make_async_remote_copy(
+            far_row, far_row, row_send.at[j], row_recv, device_id=(g, j), device_id_type=MESH
+        )
+
+    def ag_copy(k, j, c):
+        return pltpu.make_async_remote_copy(
+            chunk.at[k], gathered.at[c], ag_send.at[k, j], ag_recv.at[c],
             device_id=(g, j), device_id_type=MESH,
         )
 
@@ -284,9 +311,9 @@
         return jnp.concatenate([x, zeros], axis=0).astype(BF16)
 
     attended = []
+    for load in key_loads + value_loads:
+        load.wait()
     for r in range(slots):
-        key_loads[r].wait()
-        value_loads[r].wait()
         mine = slice(r * steps, (r + 1) * steps)
         mixed = attend(
             stack_heads(by_slot[mine], heads).astype(BF16),
@@ -317,6 +344,8 @@
 
     def put_moved(c, block):
         piece = jnp.concatenate([block[:, :LANES], block[:, LANES:]], axis=0).astype(BF16)
+        if far:
+            far_part[c] = piece
         if c < 8:
             moved_part[c, 0] = piece
         else:
@@ -338,46 +367,51 @@
         return jnp.where(has_send, moved, 0.0).astype(BF16)
 
     def send_all(parts, moved):
-        for j in reversed(range(n_t)):
+        for c in reversed(range(n_t)):
+            o = adder[c]
             if moved:
 
-                @when(near_src, j <= rank)
+                @when(near_src, o <= rank)
                 def _():
-                    mv_copy(j, t).start()
+                    mv_copy(c, t).start()
 
             if parts:
 
-                @when(rank_of(g, j) < rank)
+                @when(rank_of(g, o) < rank)
                 def _():
-                    rs_copy(j, t).start()
-
-        for j in list(range(1, n_t)) + [0]:
+                    rs_copy(c, t).start()
+
+        for o in list(range(1, n_t - 1)) + [0]:
+            own = [c for c in range(n_t) if adder[c] == o]
             if moved:
 
-                @when(near_src, j > rank)
+                @when(near_src, o > rank)
                 def _():
-                    pl.semaphore_wait(ready.at[j], 1)
-                    mv_copy(j, t).start()
+                    pl.semaphore_wait(ready.at[o], 1)
+                    for c in own:
+                        mv_copy(c, t).start()
 
             if parts:
 
-                @when(rank_of(g, j) > rank)
+                @when(rank_of(g, o) > rank)
                 def _():
-                    pl.semaphore_wait(here.at[j], 1)
-                    rs_copy(j, t).start()
+                    pl.semaphore_wait(here.at[o], 1)
+                    for c in own:
+                        rs_copy(c, t).start()
 
         if moved and far:
 
             @when(far_src_first)
             def _():
-                for j in range(n_t):
-                    pl.semaphore_wait(ready.at[j], 1)
-                    mv_copy(j, t).start()
+                for o in range(n_t - 1):
+                    pl.semaphore_wait(ready.at[o], 1)
+                    for c in range(n_t):
+                        if adder[c] == o:
+                            mv_copy(c, t).start()
 
             @when(far_src_last)
             def _():
-                for j in range(n_t):
-                    mv_copy(j, t).start()
+                far_copy(t).start()
 
     if far:
         for c in range(10):
@@ -424,53 +458,77 @@
                 put_part(c, dot(attended, columns(c)))
             send_all(True, False)
 
-    reduced[t] = part[t]
-    for j in range(n_t):
-
-        @pl.when(t != j)
-        def _():
-            rs_copy(j, j).wait_recv()
-
-    acc = reduced[0].astype(F32)
-    for j in range(1, n_t):
-        acc = acc + reduced[j].astype(F32)
-    total[...] = acc
-
-    @pl.when(is_dst)
+    i, j = grid_ids((rows, steps))
+    place = one_hot(jnp.logical_and(lax.rem(i, slots) == arrival_slot, i // slots == j))
+    takes_moved = jnp.logical_and(is_dst, jnp.logical_not(far_dst_first)) if far else is_dst
+
+    def finish(k, c, sender):
+        reduced[k, t] = part[c]
+        for j in range(n_t):
+
+            @when(j != t)
+            def _():
+                rs_copy(sender, j).wait_recv()
+
+        acc = reduced[k, 0].astype(F32)
+        for j in range(1, n_t):
+            acc = acc + reduced[k, j].astype(F32)
+        total[...] = acc
+
+        @when(takes_moved)
+        def _():
+            for j in range(n_t):
+                mv_copy(sender, j).wait_recv()
+            arrived = moved_in[k, 0].astype(F32)
+            for j in range(1, n_t):
+                arrived = arrived + moved_in[k, j].astype(F32)
+            arrived = jnp.where(has_arrival, arrived, 0.0).astype(BF16)
+            lo = dot(place, arrived[0, :steps])
+            hi = dot(place, arrived[0, steps:])
+            extra = dot(
+                place,
+                jnp.where(lax.rem(c // 2, 2) == 0, arrived[1, :steps], arrived[1, steps:]),
+            )
+            extra = jnp.where(lax.rem(c, 2) == 0, extra[:half], extra[half:])
+            total[0] += lo[:half]
+            total[1] += lo[half:]
+            total[2] += hi[:half]
+            total[3] += hi[half:]
+            total[4] += extra
+
+        chunk[k] = total[...].astype(BF16)
+        gathered[c] = chunk[k]
+        for j in range(n_t - 1):
+
+            @when(j != t)
+            def _():
+                ag_copy(k, j, c).start()
+
+    @when(t == HELPER)
     def _():
-        for j in range(n_t):
-            mv_copy(j, j).wait_recv()
-        arrived = moved_in[0].astype(F32)
-        for j in range(1, n_t):
-            arrived = arrived + moved_in[j].astype(F32)
-        arrived = jnp.where(has_arrival, arrived, 0.0).astype(BF16)
-        i, j = grid_ids((rows, steps))
-        place = one_hot(jnp.logical_and(lax.rem(i, slots) == arrival_slot, i // slots == j))
-        lo = dot(place, arrived[0, :steps])
-        hi = dot(place, arrived[0, steps:])
-        extra = dot(
-            place, jnp.where(lax.rem(t // 2, 2) == 0, arrived[1, :steps], arrived[1, steps:])
-        )
-        extra = jnp.where(lax.rem(t, 2) == 0, extra[:half], extra[half:])
-        total[0] += lo[:half]
-        total[1] += lo[half:]
-        total[2] += hi[:half]
-        total[3] += hi[half:]
-        total[4] += extra
-
-    chunk[...] = total[...].astype(BF16)
-    for j in range(n_t):
-
-        @pl.when(t != j)
-        def _():
-            ag_copy(j, t).start()
-
-    gathered[t] = chunk[...]
-    for j in range(n_t):
-
-        @pl.when(t != j)
-        def _():
-            ag_copy(j, j).wait_recv()
+        finish(1, n_t - 1, n_t - 1)
+
+    @when(t < n_t - 1)
+    def _():
+        finish(0, t, 0)
+
+    @when(rank < n_t - 1)
+    def _():
+        pl.semaphore_wait(here.at[n_t - 1], 1)
+
+    @when(t < n_t - 1)
+    def _():
+        ag_copy(0, n_t - 1, t).start()
+
+    @when(t == HELPER)
+    def _():
+        ag_copy(1, n_t - 1, n_t - 1).start()
+
+    for c in range(n_t):
+
+        @when(t != adder[c])
+        def _():
+            ag_copy(0, 0, c).wait_recv()
 
     for j in range(n_t):
         for k in range(2):
@@ -482,14 +540,62 @@
         h = j % 2
         out[h * half : (h + 1) * half, tile * LANES : (tile + 1) * LANES] = gathered[j, 4]
 
+    if far:
+
+        @when(adds)
+        def _():
+            for j in range(n_t):
+                far_copy(j).wait_recv()
+            arrived = far_in[0].astype(F32)
+            for j in range(1, n_t):
+                arrived = arrived + far_in[j].astype(F32)
+            far_row[...] = jnp.where(has_arrival, arrived, 0.0).astype(BF16)
+
+        @when(far_dst_first, jnp.logical_not(adds))
+        def _():
+            row_copy(0).wait_recv()
+
+        for spot, followers in tree.items():
+
+            @when(far_dst_first, my_place == spot)
+            def _():
+                for j in followers:
+                    row_copy(place_in_tree(j)).start()
+
+        @when(far_dst_first)
+        def _():
+            for c in range(10):
+                pair = jnp.concatenate([far_row[c, :steps], far_row[c, steps:]], axis=1)
+                out[:, 256 * c : 256 * (c + 1)] += dot(place, pair).astype(BF16)
+
+        for spot, followers in tree.items():
+
+            @when(far_dst_first, my_place == spot)
+            def _():
+                for j in followers:
+                    row_copy(place_in_tree(j)).wait_send()
+
     for j in range(n_t):
 
-        @pl.when(t != j)
+        @when(t != adder[j])
         def _():
             rs_copy(j, t).wait_send()
-            ag_copy(j, t).wait_send()
-
-    @pl.when(is_src)
+
+        @when(t != j, t < n_t - 1)
+        def _():
+            ag_copy(0, j, t).wait_send()
+
+        @when(t != j, t == HELPER)
+        def _():
+            ag_copy(1, j, n_t - 1).wait_send()
+
+    if far:
+
+        @when(far_src_last)
+        def _():
+            far_copy(t).wait_send()
+
+    @when(is_src, jnp.logical_not(far_src_last) if far else True)
     def _():
         for j in range(n_t):
             mv_copy(j, t).wait_send()
@@ -534,6 +640,7 @@
     asks = ((heads + 2) * steps, HD)
     pieces = (n_t, 5, rows // 2, LANES)
     moved = (n_t, 2, 2 * steps, LANES)
+    far = (features // (2 * LANES), 2 * steps, LANES)
     return pl.pallas_call(
         functools.partial(
             kernel, slots=slots, steps=steps, heads=heads, n_dp=n_dp, n_t=n_t, parity=parity
@@ -555,14 +662,18 @@
             pltpu.VMEM(asks, BF16),
             pltpu.VMEM((n_t,) + asks, BF16),
             pltpu.VMEM(pieces, BF16),
-            pltpu.VMEM(pieces, BF16),
+            pltpu.VMEM((2,) + pieces, BF16),
             pltpu.VMEM(moved, BF16),
-            pltpu.VMEM(moved, BF16),
+            pltpu.VMEM((2,) + moved, BF16),
+            pltpu.VMEM(far, BF16),
+            pltpu.VMEM((n_t,) + far, BF16),
+            pltpu.VMEM(far, BF16),
             pltpu.VMEM(pieces[1:], F32),
-            pltpu.VMEM(pieces[1:], BF16),
+            pltpu.VMEM((2,) + pieces[1:], BF16),
             pltpu.VMEM(pieces, BF16),
             dma((6 + 2 * slots + 10,)), dma, dma, dma((n_t,)), dma((n_t,)),
-            dma((n_t,)), dma((n_t,)), dma((n_t,)), dma((n_t,)), dma((n_t,)), dma((n_t,)),
+            dma((n_t,)), dma((2, n_t)), dma((n_t,)), dma((2, n_t)), dma((2, n_t)), dma((n_t,)),
+            dma, dma((n_t,)), dma((n_t,)), dma,
             regular((n_t,)), regular((n_t,)), regular((n_t,)),
         ],
         compiler_params=pltpu.CompilerParams(

time: 49.7 us -> 44.7 us (0.90)
  the two profiles are of different devices: /device:TPU:32 before, /device:TPU:192 now
where the time goes in v4:
time: 44.7 us; the launch traced here: 44.5 us
  Pallas kernels  43.1 us (96%)
  local copies, waits for them, and re-layouts  0.71 us (2%)
  between operations  0.67 us (1%)
    pallas_call x1, Pallas kernels, project(): pl.pallas_call(functools.partial(kernel, slots=slots, steps=steps, heads=...  41.9 us
    pallas_call x1, Pallas kernels, source_parity(): pl.pallas_call(parity_kernel, out_shape=jax.ShapeDtypeStruct((1,), jnp.in...  1.22 us

profile of v4, /device:TPU:192, one launch (start us, length us, event | category | flops | bytes accessed | tf_op | source)
XLA Modules:
  0.0 44.5 jit_solution(3326031307079025208)
XLA Ops:
  0.0 1.2 %shard_map.93 = s32[1]{0:T(128)} custom-call(s32[4,64]{1,0:T(4,128)} %bitcast.2), custom_call_target="tpu_custom_call" | custom-call | tf_op jit(solution)/shard_map/pallas_call | solution.py:623
  1.9 42.0 %conditional.1 = (bf16[8,4,2560]{2,1,0:T(4,128)(2,1)S(1)}) conditional(s32[]{:T(128)} %bitcast.1, (s32[4]{0:T(128)}, s32[4]{0:T(128)}, s32[4,64]{1,0:T(4,128)}, bf16[8,4,1024]{2,1,0:T(4,128)(2,1)}, bf16[8,4,128]{2,1,0:T(4,128)(2,1)}, /*index=5*/bf16[8,4,128]{2,1,0:T(4,128)(2,1)}, bf16[4,1536,128]{2,1,0:T(8,128)(2,1)}, ...), branch_computations={%region_0.0_spmd, %region_1.0_spmd} | conditional | bytes 327688 | solution.py:689
  1.9 41.9 %branch_0_fun.1 = bf16[32,2560]{1,0:T(8,128)(2,1)S(1)} custom-call(s32[4]{0:T(128)} %get-tuple-element.45.lengths_hbm, s32[4]{0:T(128)} %get-tuple-element.46.finished_hbm, s32[4,64]{1,0:T(4,128)} %get-tuple-element.47.mig_hbm, bf16[8,4,1024]{2,1,0:T(4,128)(2,1)} %get-tuple-element.48.query_hbm, bf16[8,4,128]{2,1,0:T(4,128)(2,1)} %get-tuple-element.49.new_keys_hbm, ...), custom_call_target="tpu_custom_call" | custom-call | tf_op jit(solution)/shard_map/cond/branch_0_fun/pallas_call | solution.py:644
  43.9 0.0 copy-start
  43.9 0.7 %copy-done = bf16[8,4,2560]{2,1,0:T(4,128)(2,1)} copy-done((bf16[8,4,2560]{2,1,0:T(4,128)(2,1)}, bf16[8,4,2560]{2,1,0:T(4,128)(2,1)S(1)}, u32[]{:S(2)}) %copy-start) | copy-done | bytes 163864
  (1 shorter events, 0.0 us)
Async XLA Ops:
  43.9 0.7 %copy-start = (bf16[8,4,2560]{2,1,0:T(4,128)(2,1)}, bf16[8,4,2560]{2,1,0:T(4,128)(2,1)S(1)}, u32[]{:S(2)}) copy-start(bf16[8,4,2560]{2,1,0:T(4,128)(2,1)S(1)} %get-tuple-element.66) | copy-start | bytes 491524

commit v5 on v4

--- a/solution.py
+++ b/solution.py
@@ -10,7 +10,7 @@
 HD = 128
 BLOCK = 512
 LANES = 128
-HELPER = 3
+BLOCK_ORDER = (8, 9, 7, 6, 5, 4, 3, 2, 1, 0)
 MESH = pl.DeviceIdType.MESH
 F32 = jnp.float32
 BF16 = jnp.bfloat16
@@ -63,10 +63,11 @@
     keys_hbm, values_hbm, weight_hbm,
     out,
     lengths, finished, mig, query, new_keys, new_values, keys, values, weight,
-    ask, asked, relay, part, reduced, moved_part, moved_in, far_part, far_in, far_row, total, chunk,
+    ask, asked, relay, part, reduced, moved_part, moved_in, far_part, far_in, far_row, back, returned,
+    rows_in, total, chunk,
     gathered,
     load_sem, ask_send, ask_recv, relay_send, relay_recv,
-    rs_send, rs_recv, mv_send, mv_recv, ag_send, ag_recv, far_send, far_recv, row_send, row_recv,
+    rs_send, rs_recv, mv_send, mv_recv, ag_send, ag_recv, far_send, far_recv, row_send, row_recv, back_send, back_recv,
     here, ready, open_sem,
     *, slots, steps, heads, n_dp, n_t, parity,
 ):
@@ -105,7 +106,7 @@
     pairs += [(values_hbm.at[r], values.at[r]) for r in range(slots)]
     pairs += [
         (weight_hbm.at[:, pl.ds(256 * c, 256)], weight.at[:, pl.ds(256 * c, 256)])
-        for c in range(10)
+        for c in BLOCK_ORDER
     ]
     loads = [
         pltpu.make_async_copy(src, dst, load_sem.at[i]) for i, (src, dst) in enumerate(pairs)
@@ -190,9 +191,11 @@
         def _():
             tell(here.at[t], g, j)
 
-        @when(near_dst, rank_of(down, j) < t, t != n_t - 1)
-        def _():
-            tell(ready.at[t], down, j)
+        if far:
+
+            @when(near_dst, rank_of(down, j) < t, t != n_t - 1)
+            def _():
+                tell(ready.at[t], down, j)
 
     ask_later = jnp.logical_and(g == 1, t == 0)
     if far:
@@ -229,19 +232,23 @@
             device_id=(relay_src, j), device_id_type=MESH,
         )
 
-    adder = list(range(n_t - 1)) + [HELPER]
-    side = [0] * (n_t - 1) + [1]
+    adders = n_t - 1 if far else n_t
 
     def rs_copy(c, slot):
         return pltpu.make_async_remote_copy(
-            part.at[c], reduced.at[side[c], slot], rs_send.at[c], rs_recv.at[side[c], slot],
-            device_id=(g, adder[c]), device_id_type=MESH,
+            part.at[c], reduced.at[slot], rs_send.at[c], rs_recv.at[slot],
+            device_id=(g, c), device_id_type=MESH,
         )
 
     def mv_copy(c, slot):
         return pltpu.make_async_remote_copy(
-            moved_part.at[c], moved_in.at[side[c], slot], mv_send.at[c],
-            mv_recv.at[side[c], slot], device_id=(up, adder[c]), device_id_type=MESH,
+            moved_part.at[c], moved_in.at[slot], mv_send.at[c], mv_recv.at[slot],
+            device_id=(up, c), device_id_type=MESH,
+        )
+
+    def back_copy(group):
+        return pltpu.make_async_remote_copy(
+            back, returned, back_send, back_recv, device_id=(group, t), device_id_type=MESH
         )
 
     def far_copy(slot):
@@ -262,9 +269,9 @@
             far_row, far_row, row_send.at[j], row_recv, device_id=(g, j), device_id_type=MESH
         )
 
-    def ag_copy(k, j, c):
-        return pltpu.make_async_remote_copy(
-            chunk.at[k], gathered.at[c], ag_send.at[k, j], ag_recv.at[c],
+    def ag_copy(j, c):
+        return pltpu.make_async_remote_copy(
+            chunk, gathered.at[c], ag_send.at[j], ag_recv.at[c],
             device_id=(g, j), device_id_type=MESH,
         )
 
@@ -310,51 +317,6 @@
     def pad(x):
         return jnp.concatenate([x, zeros], axis=0).astype(BF16)
 
-    attended = []
-    for load in key_loads + value_loads:
-        load.wait()
-    for r in range(slots):
-        mine = slice(r * steps, (r + 1) * steps)
-        mixed = attend(
-            stack_heads(by_slot[mine], heads).astype(BF16),
-            keys[r], values[r],
-            pad(fresh_by_slot[mine, :HD]), pad(fresh_by_slot[mine, HD:]),
-            lengths[r] * BLOCK, steps, heads,
-        )
-        stays = jnp.logical_and(
-            finished[r] == 0, jnp.logical_not(jnp.logical_and(has_send, sent_row == r))
-        )
-        attended.append(jnp.where(stays, mixed, 0.0))
-    attended = jnp.concatenate(attended, axis=0).astype(BF16)
-    i, j = grid_ids((rows, rows))
-    to_steps = one_hot(j == lax.rem(i, slots) * steps + i // slots)
-    attended = dot(to_steps, attended).astype(BF16)
-
-    half = rows // 2
-
-    def put_part(c, block):
-        block = block.astype(BF16)
-        for k in range(2):
-            for h in range(2):
-                piece = block[h * half : (h + 1) * half, k * LANES : (k + 1) * LANES]
-                if c < 8:
-                    part[c, 2 * k + h] = piece
-                else:
-                    part[2 * (2 * (c - 8) + k) + h, 4] = piece
-
-    def put_moved(c, block):
-        piece = jnp.concatenate([block[:, :LANES], block[:, LANES:]], axis=0).astype(BF16)
-        if far:
-            far_part[c] = piece
-        if c < 8:
-            moved_part[c, 0] = piece
-        else:
-            for j in range(4):
-                moved_part[4 * (c - 8) + j, 1] = piece
-
-    def columns(c):
-        return weight[:, 256 * c : 256 * (c + 1)]
-
     def attend_moved():
         ask_copy(g, t).wait_recv()
         asked_fresh = asked[heads * steps :, :].astype(F32)
@@ -364,60 +326,137 @@
             pad(asked_fresh[:steps]), pad(asked_fresh[steps:]),
             lengths[sent_row] * BLOCK, steps, heads,
         )
-        return jnp.where(has_send, moved, 0.0).astype(BF16)
+        return jnp.where(has_send, moved, 0.0)
+
+    attended = []
+    for load in key_loads + value_loads:
+        load.wait()
+    for r in range(slots):
+        if r in (0, slots // 2) and not far:
+            @when(is_src, last if r == 0 else jnp.logical_not(last))
+            def _():
+                back[...] = stack_heads(attend_moved(), heads).astype(BF16)
+                back_copy(up).start()
+
+        mine = slice(r * steps, (r + 1) * steps)
+        mixed = attend(
+            stack_heads(by_slot[mine], heads).astype(BF16),
+            keys[r], values[r],
+            pad(fresh_by_slot[mine, :HD]), pad(fresh_by_slot[mine, HD:]),
+            lengths[r] * BLOCK, steps, heads,
+        )
+        stays = jnp.logical_and(
+            finished[r] == 0, jnp.logical_not(jnp.logical_and(has_send, sent_row == r))
+        )
+        attended.append(jnp.where(stays, mixed, 0.0))
+    attended = jnp.concatenate(attended, axis=0)
+    if not far:
+        rows_in[...] = attended
+
+        @when(ask_later)
+        def _():
+            pl.semaphore_wait(ready.at[0], 1)
+            ask_copy(down, t).start()
+
+        @when(is_dst)
+        def _():
+            back_copy(down).wait_recv()
+            row = returned[...].astype(F32)
+            row = jnp.concatenate([row[h * steps : (h + 1) * steps] for h in range(heads)], axis=1)
+            for r in range(slots):
+                mine = slice(r * steps, (r + 1) * steps)
+                here_now = jnp.logical_and(has_arrival, arrival_slot == r)
+                rows_in[mine, :] = jnp.where(here_now, row, rows_in[mine, :])
+
+        attended = rows_in[...]
+    attended = attended.astype(BF16)
+    i, j = grid_ids((rows, rows))
+    to_steps = one_hot(j == lax.rem(i, slots) * steps + i // slots)
+    attended = dot(to_steps, attended).astype(BF16)
+
+    half = rows // 2
+
+    def home_of(c, k, h):
+        if c < adders:
+            return c, 2 * k + h
+        if far and c == adders:
+            return 2 * k + h, 5
+        n = 2 * (2 * (c - n_t) + k) + h
+        return (n, 4) if n < adders else (4, 5)
+
+    def put_part(c, block):
+        block = block.astype(BF16)
+        for k in range(2):
+            for h in range(2):
+                piece = block[h * half : (h + 1) * half, k * LANES : (k + 1) * LANES]
+                n, m = home_of(c, k, h)
+                part[n, m] = piece
+
+    for c in (5, 6) if far else ():
+        part[c, 5] = jnp.zeros(part.shape[2:], BF16)
+
+    def put_moved(c, block):
+        piece = jnp.concatenate([block[:, :LANES], block[:, LANES:]], axis=0).astype(BF16)
+        if far:
+            far_part[c] = piece
+        if c < adders:
+            moved_part[c, 0] = piece
+        elif c == adders:
+            for j in range(adders):
+                moved_part[j, 2] = piece
+        else:
+            for j in range(4 * (c - 8), min(4 * (c - 7), adders)):
+                moved_part[j, 1] = piece
+
+    def columns(c):
+        return weight[:, 256 * c : 256 * (c + 1)]
 
     def send_all(parts, moved):
-        for c in reversed(range(n_t)):
-            o = adder[c]
+        for c in reversed(range(adders)):
             if moved:
 
-                @when(near_src, o <= rank)
+                @when(near_src, c <= rank)
                 def _():
                     mv_copy(c, t).start()
 
+        for c in list(range(1, adders)) + [0]:
+            if moved:
+
+                @when(near_src, c > rank)
+                def _():
+                    pl.semaphore_wait(ready.at[c], 1)
+                    mv_copy(c, t).start()
+
             if parts:
 
-                @when(rank_of(g, o) < rank)
+                @when(rank_of(g, c) > rank)
                 def _():
+                    pl.semaphore_wait(here.at[c], 1)
                     rs_copy(c, t).start()
 
-        for o in list(range(1, n_t - 1)) + [0]:
-            own = [c for c in range(n_t) if adder[c] == o]
-            if moved:
-
-                @when(near_src, o > rank)
-                def _():
-                    pl.semaphore_wait(ready.at[o], 1)
-                    for c in own:
-                        mv_copy(c, t).start()
-
-            if parts:
-
-                @when(rank_of(g, o) > rank)
-                def _():
-                    pl.semaphore_wait(here.at[o], 1)
-                    for c in own:
-                        rs_copy(c, t).start()
-
         if moved and far:
 
             @when(far_src_first)
             def _():
-                for o in range(n_t - 1):
-                    pl.semaphore_wait(ready.at[o], 1)
-                    for c in range(n_t):
-                        if adder[c] == o:
-                            mv_copy(c, t).start()
+                for c in range(adders):
+                    pl.semaphore_wait(ready.at[c], 1)
+                    mv_copy(c, t).start()
 
             @when(far_src_last)
             def _():
                 far_copy(t).start()
 
+    for load, c in zip(weight_loads, BLOCK_ORDER):
+        load.wait()
+        put_part(c, dot(attended, columns(c)))
+        if c < adders:
+            @when(rank_of(g, c) < rank)
+            def _():
+                rs_copy(c, t).start()
+
+    send_all(True, False)
+
     if far:
-        for c in range(10):
-            weight_loads[c].wait()
-            put_part(c, dot(attended, columns(c)))
-        send_all(True, False)
 
         @when(relays)
         def _():
@@ -428,117 +467,82 @@
 
         @when(is_src)
         def _():
-            moved = attend_moved()
+            moved = attend_moved().astype(BF16)
             for c in range(10):
                 put_moved(c, dot(moved, columns(c)))
             send_all(False, True)
 
-    else:
-
-        @when(is_src)
-        def _():
-            both = jnp.concatenate([attended.astype(F32), attend_moved().astype(F32)], axis=0)
-            both = both.astype(BF16)
-            for c in range(10):
-                weight_loads[c].wait()
-                block = dot(both, columns(c))
-                put_part(c, block[:rows])
-                put_moved(c, block[rows:])
-            send_all(True, True)
-
-        @when(ask_later)
-        def _():
-            pl.semaphore_wait(ready.at[0], 1)
-            ask_copy(down, t).start()
-
-        @when(is_dst)
-        def _():
-            for c in range(10):
-                weight_loads[c].wait()
-                put_part(c, dot(attended, columns(c)))
-            send_all(True, False)
-
     i, j = grid_ids((rows, steps))
     place = one_hot(jnp.logical_and(lax.rem(i, slots) == arrival_slot, i // slots == j))
-    takes_moved = jnp.logical_and(is_dst, jnp.logical_not(far_dst_first)) if far else is_dst
-
-    def finish(k, c, sender):
-        reduced[k, t] = part[c]
+
+    @when(t < adders)
+    def _():
+        reduced[t] = part[t]
         for j in range(n_t):
 
             @when(j != t)
             def _():
-                rs_copy(sender, j).wait_recv()
-
-        acc = reduced[k, 0].astype(F32)
+                rs_copy(0, j).wait_recv()
+
+        acc = reduced[0].astype(F32)
         for j in range(1, n_t):
-            acc = acc + reduced[k, j].astype(F32)
+            acc = acc + reduced[j].astype(F32)
         total[...] = acc
 
-        @when(takes_moved)
-        def _():
+        def add_moved():
             for j in range(n_t):
-                mv_copy(sender, j).wait_recv()
-            arrived = moved_in[k, 0].astype(F32)
+                mv_copy(0, j).wait_recv()
+            arrived = moved_in[0].astype(F32)
             for j in range(1, n_t):
-                arrived = arrived + moved_in[k, j].astype(F32)
+                arrived = arrived + moved_in[j].astype(F32)
             arrived = jnp.where(has_arrival, arrived, 0.0).astype(BF16)
+            odd = lax.rem(t, 2) == 1
             lo = dot(place, arrived[0, :steps])
             hi = dot(place, arrived[0, steps:])
-            extra = dot(
-                place,
-                jnp.where(lax.rem(c // 2, 2) == 0, arrived[1, :steps], arrived[1, steps:]),
-            )
-            extra = jnp.where(lax.rem(c, 2) == 0, extra[:half], extra[half:])
+            fifth = jnp.where(lax.rem(t // 2, 2) == 0, arrived[1, :steps], arrived[1, steps:])
+            fifth = dot(place, fifth)
+            sixth = jnp.where(t < 2, arrived[2, :steps], arrived[2, steps:])
+            sixth = dot(place, jnp.where(t == 4, arrived[1, steps:], sixth))
             total[0] += lo[:half]
             total[1] += lo[half:]
             total[2] += hi[:half]
             total[3] += hi[half:]
-            total[4] += extra
-
-        chunk[k] = total[...].astype(BF16)
-        gathered[c] = chunk[k]
-        for j in range(n_t - 1):
+            total[4] += jnp.where(odd, fifth[half:], fifth[:half])
+            total[5] += jnp.where(jnp.logical_or(odd, t == 4), sixth[half:], sixth[:half])
+
+        if far:
+            when(is_dst, jnp.logical_not(far_dst_first))(add_moved)
+        chunk[...] = total[...].astype(BF16)
+        gathered[t] = chunk[...]
+        for j in range(adders):
 
             @when(j != t)
             def _():
-                ag_copy(k, j, c).start()
-
-    @when(t == HELPER)
-    def _():
-        finish(1, n_t - 1, n_t - 1)
-
-    @when(t < n_t - 1)
-    def _():
-        finish(0, t, 0)
-
-    @when(rank < n_t - 1)
-    def _():
-        pl.semaphore_wait(here.at[n_t - 1], 1)
-
-    @when(t < n_t - 1)
-    def _():
-        ag_copy(0, n_t - 1, t).start()
-
-    @when(t == HELPER)
-    def _():
-        ag_copy(1, n_t - 1, n_t - 1).start()
-
-    for c in range(n_t):
-
-        @when(t != adder[c])
-        def _():
-            ag_copy(0, 0, c).wait_recv()
-
-    for j in range(n_t):
+                ag_copy(j, t).start()
+
+    if far:
+
+        @when(rank < n_t - 1)
+        def _():
+            pl.semaphore_wait(here.at[n_t - 1], 1)
+
+        @when(t < adders)
+        def _():
+            ag_copy(n_t - 1, t).start()
+
+    for c in range(adders):
+
+        @when(t != c)
+        def _():
+            ag_copy(0, c).wait_recv()
+
+    for c in range(10):
         for k in range(2):
             for h in range(2):
-                out[h * half : (h + 1) * half, (2 * j + k) * LANES : (2 * j + k + 1) * LANES] = (
-                    gathered[j, 2 * k + h]
+                n, m = home_of(c, k, h)
+                out[h * half : (h + 1) * half, (2 * c + k) * LANES : (2 * c + k + 1) * LANES] = (
+                    gathered[n, m]
                 )
-        tile = 2 * n_t + j // 2
-        h = j % 2
-        out[h * half : (h + 1) * half, tile * LANES : (tile + 1) * LANES] = gathered[j, 4]
 
     if far:
 
@@ -577,17 +581,15 @@
 
     for j in range(n_t):
 
-        @when(t != adder[j])
-        def _():
-            rs_copy(j, t).wait_send()
-
-        @when(t != j, t < n_t - 1)
-        def _():
-            ag_copy(0, j, t).wait_send()
-
-        @when(t != j, t == HELPER)
-        def _():
-            ag_copy(1, j, n_t - 1).wait_send()
+        @when(t != j, t < adders)
+        def _():
+            ag_copy(j, t).wait_send()
+
+    for c in range(adders):
+
+        @when(t != c)
+        def _():
+            rs_copy(c, t).wait_send()
 
     if far:
 
@@ -595,10 +597,16 @@
         def _():
             far_copy(t).wait_send()
 
-    @when(is_src, jnp.logical_not(far_src_last) if far else True)
-    def _():
-        for j in range(n_t):
-            mv_copy(j, t).wait_send()
+        @when(is_src, jnp.logical_not(far_src_last))
+        def _():
+            for c in range(adders):
+                mv_copy(c, t).wait_send()
+
+    else:
+
+        @when(is_src)
+        def _():
+            back_copy(up).wait_send()
 
     @pl.when(is_dst)
     def _():
@@ -638,8 +646,10 @@
     dma = pltpu.SemaphoreType.DMA
     regular = pltpu.SemaphoreType.REGULAR
     asks = ((heads + 2) * steps, HD)
-    pieces = (n_t, 5, rows // 2, LANES)
-    moved = (n_t, 2, 2 * steps, LANES)
+    pieces = (n_t, 6 if parity else 5, rows // 2, LANES)
+    parts = (n_t - 1 if parity else n_t,) + pieces[1:]
+    moved = (n_t, 3, 2 * steps, LANES)
+    moved_parts = (n_t - 1,) + moved[1:]
     far = (features // (2 * LANES), 2 * steps, LANES)
     return pl.pallas_call(
         functools.partial(
@@ -661,19 +671,22 @@
             pltpu.VMEM(asks, BF16),
             pltpu.VMEM(asks, BF16),
             pltpu.VMEM((n_t,) + asks, BF16),
+            pltpu.VMEM(parts, BF16),
             pltpu.VMEM(pieces, BF16),
-            pltpu.VMEM((2,) + pieces, BF16),
+            pltpu.VMEM(moved_parts, BF16),
             pltpu.VMEM(moved, BF16),
-            pltpu.VMEM((2,) + moved, BF16),
             pltpu.VMEM(far, BF16),
             pltpu.VMEM((n_t,) + far, BF16),
             pltpu.VMEM(far, BF16),
+            pltpu.VMEM((heads * steps, HD), BF16),
+            pltpu.VMEM((heads * steps, HD), BF16),
+            pltpu.VMEM((rows, width), F32),
             pltpu.VMEM(pieces[1:], F32),
-            pltpu.VMEM((2,) + pieces[1:], BF16),
-            pltpu.VMEM(pieces, BF16),
+            pltpu.VMEM(pieces[1:], BF16),
+            pltpu.VMEM(parts, BF16),
             dma((6 + 2 * slots + 10,)), dma, dma, dma((n_t,)), dma((n_t,)),
-            dma((n_t,)), dma((2, n_t)), dma((n_t,)), dma((2, n_t)), dma((2, n_t)), dma((n_t,)),
-            dma, dma((n_t,)), dma((n_t,)), dma,
+            dma((n_t,)), dma((n_t,)), dma((n_t,)), dma((n_t,)), dma((n_t,)), dma((n_t,)),
+            dma, dma((n_t,)), dma((n_t,)), dma, dma, dma,
             regular((n_t,)), regular((n_t,)), regular((n_t,)),
         ],
         compiler_params=pltpu.CompilerParams(

time: 44.7 us -> 44.6 us (level)
  no operation moved by 1% of the time
where the time goes in v5:
time: 44.6 us; the launch traced here: 44.5 us
  Pallas kernels  43.1 us (97%)
  local copies, waits for them, and re-layouts  0.71 us (2%)
  between operations  0.67 us (2%)
    pallas_call x1, Pallas kernels, project(): pl.pallas_call(functools.partial(kernel, slots=slots, steps=steps, heads=...  41.8 us
    pallas_call x1, Pallas kernels, source_parity(): pl.pallas_call(parity_kernel, out_shape=jax.ShapeDtypeStruct((1,), jnp.in...  1.22 us

profile of v5, /device:TPU:192, one launch (start us, length us, event | category | flops | bytes accessed | tf_op | source)
XLA Modules:
  0.0 44.5 jit_solution(9248152577827936368)
XLA Ops:
  0.0 1.2 %shard_map.93 = s32[1]{0:T(128)} custom-call(s32[4,64]{1,0:T(4,128)} %bitcast.2), custom_call_target="tpu_custom_call" | custom-call | tf_op jit(solution)/shard_map/pallas_call | solution.py:631
  1.9 41.9 %conditional.1 = (bf16[8,4,2560]{2,1,0:T(4,128)(2,1)S(1)}) conditional(s32[]{:T(128)} %bitcast.1, (s32[4]{0:T(128)}, s32[4]{0:T(128)}, s32[4,64]{1,0:T(4,128)}, bf16[8,4,1024]{2,1,0:T(4,128)(2,1)}, bf16[8,4,128]{2,1,0:T(4,128)(2,1)}, /*index=5*/bf16[8,4,128]{2,1,0:T(4,128)(2,1)}, bf16[4,1536,128]{2,1,0:T(8,128)(2,1)}, ...), branch_computations={%region_0.0_spmd, %region_1.0_spmd} | conditional | bytes 327688 | solution.py:702
  1.9 41.8 %branch_0_fun.1 = bf16[32,2560]{1,0:T(8,128)(2,1)S(1)} custom-call(s32[4]{0:T(128)} %get-tuple-element.45.lengths_hbm, s32[4]{0:T(128)} %get-tuple-element.46.finished_hbm, s32[4,64]{1,0:T(4,128)} %get-tuple-element.47.mig_hbm, bf16[8,4,1024]{2,1,0:T(4,128)(2,1)} %get-tuple-element.48.query_hbm, bf16[8,4,128]{2,1,0:T(4,128)(2,1)} %get-tuple-element.49.new_keys_hbm, ...), custom_call_target="tpu_custom_call" | custom-call | tf_op jit(solution)/shard_map/cond/branch_0_fun/pallas_call | solution.py:654
  43.8 0.0 copy-start
  43.8 0.7 %copy-done = bf16[8,4,2560]{2,1,0:T(4,128)(2,1)} copy-done((bf16[8,4,2560]{2,1,0:T(4,128)(2,1)}, bf16[8,4,2560]{2,1,0:T(4,128)(2,1)S(1)}, u32[]{:S(2)}) %copy-start) | copy-done | bytes 163864
  (1 shorter events, 0.0 us)
Async XLA Ops:
  43.8 0.7 %copy-start = (bf16[8,4,2560]{2,1,0:T(4,128)(2,1)}, bf16[8,4,2560]{2,1,0:T(4,128)(2,1)S(1)}, u32[]{:S(2)}) copy-start(bf16[8,4,2560]{2,1,0:T(4,128)(2,1)S(1)} %get-tuple-element.66) | copy-start | bytes 491524
